TPU v7x, 128 devices: a whole 4x4x4 slice. The times are simulated.
128 devices in a mesh: row: 8 (over y, core), col: 16 (over x, z).
Axes of the slice: x: 4, y: 4, z: 4, core: 2. Of those that a mesh axis runs over, the one named last changes fastest.
Arguments:
- hess: bfloat16 [10, 8, 256, 5, 16, 256], P(None, 'row', None, None, 'col'), may hold values from -6 to 6
- coupling: float32 [128, 256, 2, 256], P(('row', 'col')), may hold values from -6 to 6
- dest_row: int32 [128, 256, 1], P(('row', 'col')), may hold values from 0 to 7, as said below
- local_row: int32 [128, 256], P(('row', 'col')), may hold values from 256 to 2559
- live: int32 [128], P(('row', 'col')), may hold values from 1 to 256, 24576 in all
- pattern: int32 [80, 80], replicated, may hold values 0 or 1
Outputs:
- factor: float32 [10, 8, 256, 5, 16, 256], P(None, 'row', None, None, 'col')
Inputs may be any that keep to these rules, and one draw needn't show every extreme that they name: `dest_row`: among one owner's 256 slots, used or not, one grid row is named exactly 64 times and no grid row more than 64 times. The first live[d] slots of owner d are used; the counts sum to 24576 and one owner uses all 256.
All inputs are finite; a program needn't handle non-finite values. No bound on the sum of `live` on one device may be relied on, other than what follows from the above.
Results may differ from a plain program's by a relative error of at most 0.0003.
Values sent between devices are 32-bit elements; how exact they have to be, the bound alone decides.
A program may use at most 192 MiB of HBM per device.

v0:
```python
import jax
import jax.numpy as jnp
from jax import lax
from jax.sharding import PartitionSpec as P


def broadcast(value, axis, source):
    kept = jnp.where(lax.axis_index(axis) == source, value, 0).astype(value.dtype)
    return lax.psum(kept, axis)


def symmetric(block):
    return jnp.tril(block) + jnp.swapaxes(jnp.tril(block, -1), -1, -2)


def right_solve(rows, lower_factor):
    return jax.scipy.linalg.solve_triangular(lower_factor, rows.T, lower=True).T


def leading(block00, block10, block11, link):
    size = block00.shape[0]
    first = symmetric(block00)
    second = symmetric(block11)
    coupled = link * block10
    whole = jnp.concatenate(
        [jnp.concatenate([first, coupled.T], 1), jnp.concatenate([coupled, second], 1)], 0
    )
    ident = jnp.eye(2 * size, dtype=whole.dtype)
    spread = jnp.sum(jnp.abs(whole), axis=1) - jnp.abs(jnp.diagonal(whole))
    whole = whole * (1.0 - ident) + ident * (1.0 + spread)[:, None]
    factor00 = jnp.linalg.cholesky(whole[:size, :size])
    factor10 = right_solve(whole[size:, :size], factor00)
    reduced = whole[size:, size:] - jnp.dot(factor10, factor10.T, precision=lax.Precision.HIGHEST)
    factor11 = jnp.linalg.cholesky(reduced)
    return (factor00, factor10, factor11)


def solve_rows(rows, lower_factor):
    result = right_solve(rows, lower_factor)
    return result


def panel_solve(block_rows, f00, f10, f11):
    first = solve_rows(block_rows[:, 0], f00)
    second = solve_rows(
        block_rows[:, 1] - jnp.dot(first, f10.T, precision=lax.Precision.HIGHEST), f11
    )
    return jnp.stack([first, second], 1)


def shards(hess, coupling, dest_row, local_row, live, pattern):
    grid_rows = lax.axis_size("row")
    grid_cols = lax.axis_size("col")
    here_row = lax.axis_index("row")
    here_col = lax.axis_index("col")
    row_blocks = hess.shape[0]
    col_blocks = hess.shape[3]
    block = hess.shape[2]
    slot_count = coupling.shape[1]
    bucket = slot_count // 4
    height = row_blocks * block
    mask = pattern.astype(jnp.float32)
    grid_ids = jnp.arange(grid_rows, dtype=jnp.int32)
    dest = dest_row[0, :, 0]
    active = jnp.arange(slot_count, dtype=jnp.int32) < live[0]
    hits = (dest[:, None] == grid_ids[None, :]) & active[:, None]
    ranks = jnp.cumsum(hits.astype(jnp.int32), axis=0) - 1
    place = jnp.sum(jnp.where(hits, ranks + grid_ids[None, :] * bucket, 0), axis=1)
    place = jnp.where(active, place, grid_rows * bucket)
    outgoing = (
        jnp.zeros((grid_rows * bucket, 2, block), jnp.float32)
        .at[place]
        .set(coupling[0], mode="drop")
    )
    labels = (
        jnp.zeros((grid_rows * bucket,), jnp.float32)
        .at[place]
        .set(local_row[0].astype(jnp.float32), mode="drop")
    )
    arrived, arrived_rows = (
        lax.all_to_all(
            outgoing.reshape(grid_rows, bucket, 2, block),
            "row",
            split_axis=0,
            concat_axis=0,
            tiled=True,
        ),
        lax.all_to_all(
            labels.reshape(grid_rows, bucket), "row", split_axis=0, concat_axis=0, tiled=True
        ),
    )
    partial_value = (
        jnp.zeros((height, 2, block), jnp.float32)
        .at[arrived_rows.astype(jnp.int32).reshape(-1)]
        .add(arrived.reshape(-1, 2, block))
    )
    own = hess[:, 0, :, 0, 0, :].astype(jnp.float32).reshape(height, block)
    which = (jnp.arange(2, dtype=jnp.int32) == here_col).astype(jnp.float32)
    partial_value = partial_value + own[:, None, :] * which[None, :, None]
    corner = hess[0, 0, :, 0, 0, :].astype(jnp.float32)
    at_first = ((here_row == 0) & (here_col == 0)).astype(jnp.float32)
    at_below = ((here_row == 1) & (here_col == 0)).astype(jnp.float32)
    at_second = ((here_row == 1) & (here_col == 1)).astype(jnp.float32)
    pivots = lax.psum(
        jnp.stack([at_first * corner, at_below * corner, at_second * corner]), ("row", "col")
    )
    f00, f10, f11 = leading(pivots[0], pivots[1], pivots[2], mask[1, 0])
    mine = lax.dynamic_index_in_dim(
        mask.reshape(row_blocks, grid_rows, -1), here_row, 1, keepdims=False
    )
    rowmask = jnp.repeat(mine[:, :2], block, axis=0)
    summed = lax.psum(partial_value, "col")
    panel = panel_solve(summed * rowmask[:, :, None], f00, f10, f11)
    head_first = jnp.where(here_row == 0, f00, f10)
    head_second = jnp.where(here_row == 0, jnp.zeros_like(f11), f11)
    head = jnp.stack([head_first, head_second], 1)
    panel = panel.at[:block].set(jnp.where(here_row < 2, head, panel[:block]))
    ratio = grid_cols // grid_rows
    picked = lax.dynamic_index_in_dim(
        panel.reshape(col_blocks, ratio, block, 2, block), here_col // grid_rows, 1, keepdims=False
    )
    across = broadcast(picked, "row", here_col % grid_rows)
    left = panel.reshape(height, 2 * block)
    right = across.reshape(col_blocks * block, 2 * block)
    update = jnp.dot(left, right.T, precision=lax.Precision.HIGHEST).reshape(
        row_blocks, block, col_blocks, block
    )
    tiles = jnp.transpose(hess[:, 0, :, :, 0, :].astype(jnp.float32), (0, 2, 1, 3))
    sym = symmetric(tiles)
    block_i = jnp.arange(row_blocks, dtype=jnp.int32) * grid_rows + here_row
    block_j = jnp.arange(col_blocks, dtype=jnp.int32) * grid_cols + here_col
    links = lax.dynamic_index_in_dim(
        lax.dynamic_index_in_dim(
            mask.reshape(row_blocks, grid_rows, col_blocks, grid_cols), here_row, 1, keepdims=False
        ),
        here_col,
        2,
        keepdims=False,
    )
    same = (block_i[:, None] == block_j[None, :])[:, :, None, None]
    below = (block_i[:, None] > block_j[None, :])[:, :, None, None]
    base = jnp.where(same, sym, jnp.where(below, links[:, :, None, None] * tiles, 0.0))
    trail = base - jnp.transpose(update, (0, 2, 1, 3))
    lower_panel = jnp.transpose(panel.reshape(row_blocks, block, 2, block), (0, 2, 1, 3))
    panel_tile = lax.dynamic_index_in_dim(lower_panel, jnp.minimum(here_col, 1), 1, keepdims=False)
    in_panel = (block_j < 2)[None, :, None, None]
    kept = (block_i[:, None] >= block_j[None, :])[:, :, None, None]
    result = jnp.where(in_panel, panel_tile[:, None], jnp.where(kept, trail, 0.0))
    return jnp.transpose(result, (0, 2, 1, 3)).reshape(row_blocks, 1, block, col_blocks, 1, block)


def solution(mesh):
    return jax.shard_map(
        shards,
        mesh=mesh,
        in_specs=(
            P(None, "row", None, None, "col", None),
            P(("row", "col"), None, None, None),
            P(("row", "col"), None, None),
            P(("row", "col"), None),
            P(("row", "col")),
            P(),
        ),
        out_specs=P(None, "row", None, None, "col", None),
        check_vma=False,
    )
```

profile of v0, /device:TPU:27, one launch (start us, length us, event | category | flops | bytes accessed | tf_op | source)
XLA Modules:
  0.0 535.1 jit_solution(3496052499015908950)
XLA Ops:
  9.6 0.7 convert_element_type.94
  10.2 0.8 fusion.45
  11.0 1.4 scatter_custom_fusion
  13.1 5.0 all-to-all-start
  18.1 1.0 fusion.18
  19.1 0.9 pad_maximum_fusion.3
  20.1 2.5 slice.121
  22.7 1.5 bitcast_convert_fusion
  24.4 4.2 broadcast_multiply_fusion.1
  28.7 9.5 %copy.92 = bf16[10,1,256,5,1,256]{2,5,3,0,4,1:T(8,128)(2,1)} copy(bf16[10,1,256,5,1,256]{5,2,4,3,1,0:T(8,128)(2,1)} %param.11) | data formatting | bytes 13107200 | tf_op args[0]
  39.0 0.8 copy.91
  40.3 1.3 broadcast_in_dim.117
  41.6 24.4 %scatter_fusion = f32[512,2,256]{2,1,0:T(2,128)} fusion(f32[512,2,256]{2,1,0:T(2,128)} %broadcast_in_dim.117, s32[256]{0:T(256)S(1)} %bitcast.213, f32[256,2,256]{2,1,0:T(2,128)S(1)} %bitcast.204), kind=kCustom, calls=%fused_computation.2 | custom fusion | bytes 1573888 | tf_op jit(solution)/shard_map/scatter | solution.py:73
  66.0 4.6 all-to-all-start.1
  70.7 101.6 %all-reduce.5.cloned.1.call-done = f32[3,256,256]{2,1,0:T(8,128)} async-done(((f32[3,256,256]{2,1,0:T(8,128)}), f32[3,256,256]{2,1,0:T(8,128)}) %all-reduce.5.cloned.1.call-update) | async-done | bytes 786448 | tf_op jit(solution)/shard_map/psum | solution.py:104
  172.3 1.1 fusion.26
  173.6 1.2 bitcast_add_fusion.3
  174.8 1.7 fusion.29
  176.8 4.5 gather_fusion
  181.7 63.4 %scatter_fusion.1 = f32[2560,2,256]{2,1,0:T(2,128)} fusion(f32[2560,2,256]{2,1,0:T(2,128)} %broadcast_multiply_fusion.1, s32[512]{0:T(512)S(1)} %bitcast.208, f32[512,2,256]{2,1,0:T(2,128)S(1)} %bitcast.203), kind=kCustom, calls=%fused_computation.3 | custom fusion | flops 262144 | bytes 3147776 | tf_op jit(solution)/shard_map/scatter-add | solution.py:95
  245.1 8.7 %copy.80 = f32[2560,2,256]{0,2,1:T(8,128)} copy(f32[2560,2,256]{2,1,0:T(2,128)} %scatter_fusion.1) | data formatting | bytes 10485760 | tf_op jit(solution)/shard_map/scatter-add | solution.py:95
  254.2 11.7 %cholesky.130 = f32[128,128]{1,0:T(8,128)S(1)} custom-call(f32[128,128]{1,0:T(8,128)S(1)} %cholesky.194), custom_call_target="Cholesky" | custom-call | tf_op jit(solution)/shard_map/jit(cholesky)/cholesky | solution.py:31
  265.9 9.8 %custom-call.20 = f32[1,128,128]{1,2,0:T(8,128)S(1)} custom-call(f32[1,128,128]{2,1,0:T(8,128)S(1)} %get-tuple-element.87), custom_call_target="InvertDiagBlocksLowerTriangular" | custom-call | tf_op jit(solution)/shard_map/jit(cholesky)/cholesky | solution.py:31
  276.2 11.7 %cholesky.147 = f32[128,128]{1,0:T(8,128)S(1)} custom-call(f32[128,128]{1,0:T(8,128)S(1)} %convolution_subtract_fusion.6), custom_call_target="Cholesky" | custom-call | tf_op jit(solution)/shard_map/jit(cholesky)/cholesky | solution.py:31
  288.0 0.7 compare_reduce_fusion.2
  290.1 4.1 while.6
  290.7 1.4 bitcast_dynamic-update-slice_fusion.4
  292.8 1.4 bitcast_dynamic-update-slice_fusion.4
  294.2 20.1 %custom-call.21 = f32[2,128,128]{1,2,0:T(8,128)S(1)} custom-call(f32[2,128,128]{2,1,0:T(8,128)S(1)} %get-tuple-element.41), custom_call_target="InvertDiagBlocksLowerTriangular" | custom-call | tf_op jit(solution)/shard_map/jit(_solve_triangular)/triangular_solve | solution.py:17
  316.0 11.7 %cholesky.164 = f32[128,128]{1,0:T(8,128)S(1)} custom-call(f32[128,128]{1,0:T(8,128)S(1)} %cholesky.197), custom_call_target="Cholesky" | custom-call | tf_op jit(solution)/shard_map/jit(cholesky)/cholesky | solution.py:34
  327.8 9.8 %custom-call.22 = f32[1,128,128]{1,2,0:T(8,128)S(1)} custom-call(f32[1,128,128]{2,1,0:T(8,128)S(1)} %get-tuple-element.83), custom_call_target="InvertDiagBlocksLowerTriangular" | custom-call | tf_op jit(solution)/shard_map/jit(cholesky)/cholesky | solution.py:34
  338.1 11.7 %cholesky.181 = f32[128,128]{1,0:T(8,128)S(1)} custom-call(f32[128,128]{1,0:T(8,128)S(1)} %convolution_subtract_fusion.5), custom_call_target="Cholesky" | custom-call | tf_op jit(solution)/shard_map/jit(cholesky)/cholesky | solution.py:34
  350.5 0.7 compare_reduce_fusion
  352.5 0.8 select_bitcast_fusion
  353.2 4.1 while.7
  353.9 1.4 bitcast_dynamic-update-slice_fusion.5
  355.9 1.4 bitcast_dynamic-update-slice_fusion.5
  357.3 20.4 %custom-call.23 = f32[2,128,128]{1,2,0:T(8,128)} custom-call(f32[2,128,128]{2,1,0:T(8,128)S(1)} %get-tuple-element.42), custom_call_target="InvertDiagBlocksLowerTriangular" | custom-call | tf_op jit(solution)/shard_map/jit(_solve_triangular)/triangular_solve | solution.py:17
  377.8 0.8 fusion.21
  378.5 3.0 broadcast_multiply_fusion
  381.7 2.2 copy-done.1
  383.9 1.3 fusion.13
  385.1 2.3 convolution_subtract_fusion.2
  387.9 3.5 fusion.42
  391.4 4.4 fusion.8
  395.9 1.3 fusion.11
  397.1 1.1 copy-done.2
  398.2 2.3 convolution_subtract_fusion.1
  400.5 2.8 copy.89
  403.5 1.1 copy-done.4
  404.7 2.4 fusion.34
  408.6 2.2 copy-done
  410.8 2.0 copy.99
  412.8 3.2 dot_general.16
  416.1 0.8 copy-done.8
  416.9 11.6 %convert_multiply_fusion = (f32[10,256,5,256]{1,3,2,0:T(8,128)}, f32[10,256,5,256]{1,3,2,0:T(8,128)}) fusion(bf16[10,1,256,5,1,256]{2,5,3,0,4,1:T(8,128)(2,1)} %copy.92, f32[10,5]{1,0:T(8,128)S(1)} %bitcast.206, pred[256,256]{0,1:T(8,128)(4,1)S(1)} %copy-done.8), kind=kLoop, calls=%fused_computation.8 | loop fusion | flops 9830400 | bytes 32833736 | tf_op jit(solution)/shard_map/mul | solution.py:142
  428.5 14.0 %copy.94 = f32[10,256,5,256]{3,1,2,0:T(8,128)} copy(f32[10,256,5,256]{1,3,2,0:T(8,128)} %get-tuple-element.67) | data formatting | bytes 26214400 | tf_op jit(solution)/shard_map/jit(tril)/select_n | solution.py:13
  442.5 14.0 %copy.97 = f32[10,256,5,256]{3,1,2,0:T(8,128)} copy(f32[10,256,5,256]{1,3,2,0:T(8,128)} %get-tuple-element.66) | data formatting | bytes 26214400 | tf_op jit(solution)/shard_map/mul | solution.py:142
  456.7 10.4 %copy.98 = f32[2560,2,256]{2,1,0:T(2,128)} copy(f32[2560,2,256]{2,0,1:T(8,128)} %copy-done) | data formatting | bytes 10485760 | tf_op jit(solution)/shard_map/scatter | solution.py:117
  467.1 8.0 %reshape.409 = f32[10,256,512,1]{2,1,0,3:T(8,128)} reshape(f32[2560,2,256]{2,1,0:T(2,128)} %copy.98) | data formatting | bytes 10485760 | tf_op jit(solution)/shard_map/dot_general | solution.py:125
  475.1 2.1 dynamic-slice_bitcast_fusion
  477.2 4.8 all-reduce.9.cloned.1.call-done
  482.0 30.4 %fusion.6 = f32[10,1,256,5,1,256]{5,2,3,0,4,1:T(8,128)S(1)} fusion(f32[10,256,5,256]{3,1,2,0:T(8,128)} %copy.94, f32[10,256,5,256]{3,1,2,0:T(8,128)} %copy.97, bf16[10,1,256,5,1,256]{2,5,3,0,4,1:T(8,128)(2,1)} %copy.92, f32[10,256,256]{2,1,0:T(8,128)S(1)} %dynamic-slice_bitcast_fusion, pred[5]{0:T(512)(128)(4,1)S(1)} %broadcast_compare_fusion.3, ...), kind=kOutput, calls=%fused_computation.17 | convolution fusion | flops 20158873600 | bytes 56426652 | tf_op jit(solution)/shard_map/dot_general | solution.py:125
  512.4 15.0 %copy.100 = f32[10,1,256,5,1,256]{5,4,3,2,1,0:T(1,128)} copy(f32[10,1,256,5,1,256]{5,2,3,0,4,1:T(8,128)S(1)} %fusion.6) | data formatting | bytes 26214400 | tf_op jit(solution)/shard_map/reshape | solution.py:149
  (109 shorter events, 13.6 us)
Async XLA Ops:
  13.1 52.9 %all-to-all-start = ((f32[8,1,64]{2,1,0:T(1,128)}), f32[8,1,64]{2,1,0:T(1,128)S(1)}, u32[]{:S(2)}, u32[]{:S(2)}) async-start(f32[8,1,64]{2,1,0:T(1,128)} %all_to_all.9), calls=%async_computation | async-start | bytes 8192 | tf_op jit(solution)/shard_map/all_to_all | solution.py:88
  18.1 154.2 %all-reduce.5.cloned.1.call-start = ((), (), s32[]{:S(2)}) async-start(), calls=%async_computation.2 | async-start | bytes 1572864 | tf_op jit(solution)/shard_map/psum | solution.py:104
  19.1 3.5 copy-start.11
  28.7 12.9 %copy-start.7 = (f32[1,256,2,256]{3,2,1,0:T(2,128)S(1)}, f32[1,256,2,256]{3,2,1,0:T(2,128)}, u32[]{:S(2)}) copy-start(f32[1,256,2,256]{3,2,1,0:T(2,128)} %param.12) | copy-start | bytes 1572868
  66.0 115.7 %all-to-all-start.1 = ((f32[8,64,2,256]{3,2,1,0:T(2,128)}), f32[8,64,2,256]{3,2,1,0:T(2,128)S(1)}, u32[]{:S(2)}, u32[]{:S(2)}) async-start(f32[8,64,2,256]{3,2,1,0:T(2,128)} %bitcast.26), calls=%async_computation.1 | async-start | bytes 2097152 | tf_op jit(solution)/shard_map/all_to_all | solution.py:81
  70.6 307.9 %all-reduce.7.cloned.1.call-start = ((), (), s32[]{:S(2)}) async-start(), calls=%async_computation.3 | async-start | bytes 10485760 | tf_op jit(solution)/shard_map/psum | solution.py:112
  253.9 228.1 %all-reduce.9.cloned.1.call-start = ((), (), s32[]{:S(2)}) async-start(), calls=%async_computation.4 | async-start | bytes 5242880 | tf_op jit(solution)/shard_map/psum | solution.py:9
  315.8 62.7 %copy-start.10 = (f32[1,2,10,256]{3,1,2,0:T(2,128)S(1)}, f32[1,2,10,256]{3,1,2,0:T(2,128)}, u32[]{:S(2)}) copy-start(f32[1,2,10,256]{3,1,2,0:T(2,128)} %copy.116) | copy-start | bytes 61444
  381.5 2.4 copy-start.1
  391.4 4.4 copy-start.9
  397.1 1.1 copy-start.2
  403.3 1.3 copy-start.4
  404.7 2.4 copy-start.3
  407.3 1.0 copy-start.5
  407.3 1.0 copy-start.6
  408.4 2.4 copy-start
  416.0 0.8 copy-start.8
Sparse Core Ops, SparseCore 0:
  24.3 147.9 all-reduce.4
  416.2 65.7 all-reduce.8
Sparse Core Ops, SparseCore 1:
  254.0 112.0 all-reduce.6
where the time goes:
time: 545 us; the launch traced here: 535 us
  other arithmetic  205 us (38%)
  local copies, waits for them, and re-layouts  145 us (27%)
  waiting for transfers between devices  106 us (19%)
  matrix products  50.3 us (9%)
  between operations  19 us (3%)
  starting transfers between devices  9.81 us (2%)
    psum x1, waiting for transfers between devices, shards(): lax.psum(jnp.stack([at_first * corner, at_below * corner, at_second * cor...  102 us
    scatter-add x1, other arithmetic, shards(): partial_value = jnp.zeros((height, 2, block), jnp.float32).at[arrived_row...  63.4 us
    another operation x5, other arithmetic, right_solve(): return jax.scipy.linalg.solve_triangular(lower_factor, rows.T, lower=True).T  40.6 us
    another operation x7, other arithmetic, leading(): factor11 = jnp.linalg.cholesky(reduced)  34.6 us
    another operation x6, other arithmetic, leading(): factor00 = jnp.linalg.cholesky(whole[:size, :size])  34 us
    dot_general x1, matrix products, shards(): jnp.dot(left, right.T, precision=lax.Precision.HIGHEST)  30.4 us
    scatter x1, local copies, waits for them, and re-layouts, shards(): outgoing = jnp.zeros((grid_rows * bucket, 2, block), jnp.float32).at[plac...  24.4 us
    unnamed x28, local copies, waits for them, and re-layouts  18.3 us
  transfers between devices with their start and end apart: 5, of which 2 were waited for; matrix products, arithmetic and copies ran while one was open for 45% of the time, Pallas kernels for 0%

commit v1 on v0

v1 whole, which is shorter than its diff:
```python
import jax
import jax.numpy as jnp
from jax import lax
from jax.experimental import pallas as pl
from jax.experimental.pallas import tpu as pltpu
from jax.sharding import PartitionSpec as P

F32 = jnp.float32
BF = jnp.bfloat16
MESH = pl.DeviceIdType.MESH
NR, NC, NX, NZ = 8, 16, 4, 4


def dotg(a, b, ca, cb, precision=lax.Precision.HIGHEST):
    return lax.dot_general(
        a, b, (((ca,), (cb,)), ((), ())), precision=precision, preferred_element_type=F32
    )


def dot1(a, b, ca, cb):
    return lax.dot_general(a, b, (((ca,), (cb,)), ((), ())), preferred_element_type=F32)


def split(x):
    hi = x.astype(BF)
    return hi, (x - hi.astype(F32)).astype(BF)


def iota(shape, dim):
    return lax.broadcasted_iota(jnp.int32, shape, dim)


def sym_block(x):
    n = x.shape[0]
    return jnp.where(iota((n, n), 0) >= iota((n, n), 1), x, x.T)


def build_g(h00, h10, h11, link, g_ref):
    g_ref[0:256, 0:256] = sym_block(h00)
    g_ref[256:512, 256:512] = sym_block(h11)
    x = h10 * link
    g_ref[256:512, 0:256] = x
    g_ref[0:256, 256:512] = x.T
    for i in range(4):
        rows = slice(i * 128, (i + 1) * 128)
        g = g_ref[rows, :]
        on = iota((128, 512), 0) + i * 128 == iota((128, 512), 1)
        s = jnp.sum(jnp.where(on, 0.0, jnp.abs(g)), axis=1, keepdims=True) + 1.0
        g_ref[rows, :] = jnp.where(on, s, g)


def panels(s_ref, lo, hi):
    lane = iota((8, 128), 1)
    sub = iota((8, 1), 0)

    def body(b, carry):
        base = pl.multiple_of(b * 8, 8)
        rows = s_ref[pl.ds(base, 8), :]
        ra = rows[:, :128]
        cs = [
            jnp.sum(jnp.where(lane == base + j, ra, 0.0), axis=1, keepdims=True)
            for j in range(8)
        ]
        invd = jnp.zeros((8, 1), F32)
        for j in range(8):
            inv = 1.0 / cs[j][j : j + 1, :]
            m = jnp.where(sub > j, cs[j] * inv, 0.0)
            invd = jnp.where(sub == j, inv, invd)
            rows = rows - m * rows[j : j + 1, :]
            for k in range(j + 1, 8):
                cs[k] = cs[k] - m * cs[k][j : j + 1, :]
        s_ref[pl.ds(base, 8), :] = rows
        um = jnp.where(lane >= base + 8, rows[:, :128], 0.0)
        s_ref[...] = s_ref[...] - dotg(um, rows * invd, 0, 0)
        return carry

    lax.fori_loop(lo, hi, body, 0)


def diag_begin(k, g_ref, s_ref):
    o = k * 128
    s_ref[:, 0:128] = g_ref[o : o + 128, o : o + 128]
    s_ref[:, 128:256] = jnp.where(iota((128, 128), 0) == iota((128, 128), 1), 1.0, 0.0)


def diag_end(k, g_ref, s_ref, l_ref, v_ref):
    o, e = k * 128, k * 128 + 128
    r, c = iota((128, 128), 0), iota((128, 128), 1)
    u = s_ref[:, 0:128]
    s = lax.rsqrt(jnp.sum(jnp.where(r == c, u, 0.0), axis=1, keepdims=True))
    l_ref[o:e, o:e] = jnp.where(r <= c, u * s, 0.0).T
    v = s_ref[:, 128:256] * s
    v_ref[o:e, o:e] = v
    if e < 512:
        lp = dotg(g_ref[e:512, o:e], v, 1, 1)
        l_ref[e:512, o:e] = lp
        l_ref[o:e, e:512] = jnp.zeros((128, 512 - e), F32)
        v_ref[o:e, e:512] = jnp.zeros((128, 512 - e), F32)
        g_ref[e:512, e:512] = g_ref[e:512, e:512] - dotg(lp, lp, 1, 1)
    if o > 0:
        t = dotg(l_ref[o:e, 0:o], v_ref[0:o, 0:o], 1, 0)
        v_ref[o:e, 0:o] = -dotg(v, t, 1, 0)


def move_kernel(
    live_ref, link_ref, dest_ref, lrow_ref, coup_ref, hcol_ref,
    oa_ref, ob_ref, ja_ref, jb_ref, l_ref, v_ref,
    pack_s, pack_r, rows_hi, rows_lo, pv, pv_src, pa, pb, ra1, rb1, ra2, rb2, own_a, own_b,
    g_ref, s_ref,
    a2a_s, a2a_r, p1_s, p1_r, p2_s, p2_r, p3_s, p3_r, rs_s, rs_r, ag_s, ag_r, y_s, y_r, loc,
):
    r = lax.axis_index("row")
    c = lax.axis_index("col")
    x, z = c // NZ, c % NZ

    def copy(src, dst, ss, rs, dev):
        return pltpu.make_async_remote_copy(
            src_ref=src, dst_ref=dst, send_sem=ss, recv_sem=rs, device_id=dev,
            device_id_type=MESH,
        )

    barrier = pltpu.get_barrier_semaphore()
    for d in range(1, NR):
        pl.semaphore_signal(barrier, 1, device_id=((r + d) % NR, c), device_id_type=MESH)
    for d in range(1, NC):
        pl.semaphore_signal(barrier, 1, device_id=(r, (c + d) % NC), device_id_type=MESH)

    pv_src[...] = hcol_ref[0].astype(F32).reshape(NC, 16, 256)

    lane = iota((1, 256), 1)
    active = lane < live_ref[0]
    dest = dest_ref[...]
    hits = jnp.where((iota((NR, 256), 0) == dest) & active, 1.0, 0.0)
    before = jnp.where(iota((256, 256), 0) <= iota((256, 256), 1), 1.0, 0.0).astype(BF)
    cum = dot1(hits.astype(BF), before, 1, 0)
    rank = jnp.sum(hits * cum, axis=0, keepdims=True).astype(jnp.int32) - 1
    place = jnp.where(active, dest * 64 + rank, -1)
    pick = jnp.where(iota((512, 256), 0) == place, 1.0, 0.0).astype(BF)
    c_hi, c_lo = split(coup_ref[...])
    packed = dot1(pick, c_hi, 1, 0) + dot1(pick, c_lo, 1, 0)
    pack_s[:, 0:64, :] = packed.reshape(NR, 64, 512)
    lr = lrow_ref[...]
    spot = jnp.where(iota((512, 256), 0) == rank + r * 64, 1.0, 0.0).astype(BF)
    lab_hi = (hits * (lr // 256).astype(F32)).astype(BF)
    lab_lo = (hits * (lr % 256).astype(F32)).astype(BF)
    labels = (
        dot1(lab_hi, spot, 1, 1) * 256.0
        + dot1(lab_lo, spot, 1, 1)
        + dot1(hits.astype(BF), spot, 1, 1)
    )
    for g in range(NR):
        pack_s[g, 64:72, :] = jnp.broadcast_to(labels[g : g + 1, :], (8, 512))

    pl.semaphore_wait(barrier, NR - 1 + NC - 1)

    sources = ((0, 0), (1, 0), (1, 1))

    def p1(b, d):
        to = (sources[b][1] + d) % NC
        return copy(pv_src.at[to], pv.at[b, to], p1_s.at[b, d], p1_r.at[b], (sources[b][0], to))

    for b, (sr, sc) in enumerate(sources):

        @pl.when((r == sr) & (c == sc))
        def _():
            for d in range(1, NC):
                p1(b, d).start()
            pv[b, sc] = pv_src[sc]

    def a2a(d):
        to = (r + d) % NR
        return copy(pack_s.at[to], pack_r.at[r], a2a_s.at[d], a2a_r.at[d], (to, c))

    for d in range(1, NR):
        a2a(d).start()
    pack_r[r] = pack_s[r]

    for b, (sr, sc) in enumerate(sources):

        @pl.when((r == sr) & (c != sc))
        def _():
            p1(b, 1).wait_recv()

    def p2(k, d):
        blocks = pl.ds(0, 1) if k == 0 else pl.ds(1, 2)
        to = (k + d) % NR
        part = pv.at[blocks, c]
        return copy(part, part, p2_s.at[k, d], p2_r.at[k], (to, c))

    for k in (0, 1):

        @pl.when(r == k)
        def _():
            for d in range(1, NR):
                p2(k, d).start()

    for k in (0, 1):

        @pl.when(r != k)
        def _():
            p2(k, 1).wait_recv()

    def p3(d):
        part = pv.at[:, c]
        return copy(part, part, p3_s.at[d], p3_r.at[d], (r, (c + d) % NC))

    for d in range(1, NC):
        p3(d).start()

    for d in range(1, NR):
        a2a(d).wait_recv()
    lab = jnp.zeros((8, 512), F32)
    for g in range(NR):
        lab = lab + pack_r[g, 64:72, :]
        hi, lo = split(pack_r[g, 0:64, :])
        rows_hi[g * 64 : (g + 1) * 64, :] = hi
        rows_lo[g * 64 : (g + 1) * 64, :] = lo
    lab = lab[0:1, :].astype(jnp.int32) - 1
    first = jnp.where(c == 0, 1.0, 0.0)
    second = jnp.where(c == 1, 1.0, 0.0)
    for p in (0, 1):

        def fill(t2, carry):
            t = t2 * 2 + p
            pick = jnp.where(iota((256, 512), 0) + t * 256 == lab, 1.0, 0.0).astype(BF)
            got = dot1(pick, rows_hi[...], 1, 0) + dot1(pick, rows_lo[...], 1, 0)
            h = hcol_ref[t].astype(F32)
            pa[p, t2] = (got[:, 0:256] + h * first).reshape(NX, NZ, 16, 256)
            pb[p, t2] = (got[:, 256:512] + h * second).reshape(NX, NZ, 16, 256)
            return carry

        lax.fori_loop(0, 5, fill, 0)

    def along_x(n):
        return (r, (n % NX) * NZ + z)

    def along_z(n):
        return (r, x * NZ + n % NZ)

    halves = (
        (
            (x, along_x, lambda n, p: pa.at[p, :, n % 4], ra1),
            (z, along_z, lambda n, p: pa.at[p, :, x, n % 4], ra2),
            (z, along_z, lambda n, p: oa_ref.at[p, :, x, n % 4]),
            (x, along_x, lambda n, p: oa_ref.at[p, :, n % 4]),
        ),
        (
            (z, along_z, lambda n, p: pb.at[p, :, :, n % 4], rb1),
            (x, along_x, lambda n, p: pb.at[p, :, n % 4, z], rb2),
            (x, along_x, lambda n, p: ob_ref.at[p, :, n % 4, z]),
            (z, along_z, lambda n, p: ob_ref.at[p, :, :, n % 4]),
        ),
    )

    def rs(half, phase, m):
        n, dev, unit, buf = halves[half][phase]
        src, to = (
            (unit(n + 2, 0), n + 1),
            (unit(n + 1, 1), n + 1),
            (unit(n + 1, 0), n + 1),
            (unit(n + 2, 1), n + 3),
            (unit(n + 3, 0), n + 3),
            (unit(n + 3, 1), n + 3),
        )[m]
        return copy(
            src, buf.at[m], rs_s.at[half, phase, m], rs_r.at[half, phase, m], dev(to)
        )

    def rs_start(half, phase):
        for m in (0, 3, 1, 4):
            rs(half, phase, m).start()

    def rs_middle(half, phase):
        n, dev, unit, buf = halves[half][phase]
        for m_in, m_out, to, p in ((0, 2, n + 1, 0), (3, 5, n + 3, 1)):
            rs(half, phase, m_in).wait_recv()
            ref = unit(to, p)
            ref[...] = ref[...] + buf[m_in]
            rs(half, phase, m_out).start()

    def rs_end(half, phase):
        n, dev, unit, buf = halves[half][phase]
        for m in (1, 4, 2, 5):
            rs(half, phase, m).wait_recv()
        for p, (m1, m2) in enumerate(((2, 4), (1, 5))):
            ref = unit(n, p)
            ref[...] = ref[...] + (buf[m1] + buf[m2])

    def rs_drain(half, phase):
        for m in range(6):
            rs(half, phase, m).wait_send()

    def ag(half, phase, m):
        n, dev, unit = halves[half][2 + phase]
        src, to = (
            (unit(n, 0), n + 1),
            (unit(n, 1), n + 1),
            (unit(n, 1), n + 3),
            (unit(n, 0), n + 3),
            (unit(n + 3, 0), n + 1),
            (unit(n + 1, 1), n + 3),
        )[m]
        return copy(src, src, ag_s.at[half, phase, m], ag_r.at[half, phase, m], dev(to))

    def ag_start(half, phase):
        for m in (0, 2, 1, 3):
            ag(half, phase, m).start()

    def ag_forward(half, phase):
        for m_in, m_out in ((0, 4), (2, 5)):
            ag(half, phase, m_in).wait_recv()
            ag(half, phase, m_out).start()

    def ag_wait(half, phase, ms):
        for m in ms:
            ag(half, phase, m).wait_recv()

    def ag_drain(half, phase):
        for m in range(6):
            ag(half, phase, m).wait_send()

    y, ys = r // 2, (c % NR) // 2
    chain = r % 2 == c % 2
    par = c // NR
    hop = ((y - ys + 4) % 4, (ys - y + 4) % 4)

    def y_refs(half, n):
        if half == 0:
            return oa_ref.at[par, :, n % 4], ja_ref.at[:, n % 4]
        return ob_ref.at[par, :, :, n % 4], jb_ref.at[:, :, n % 4]

    def y_copy(half, n, k, i, from_o):
        o, j = y_refs(half, n)
        step = 2 if half == 0 else 6
        to = ((r + step) % NR, c) if i == 0 else (r + 1 - 2 * (r % 2), c)
        return copy(o if from_o else j, j, y_s.at[half, k, i], y_r.at[half, k], to)

    def y_local(half, n, k):
        o, j = y_refs(half, n)
        return pltpu.make_async_copy(o, j, loc.at[half, k])

    def y_source(half, n, k):
        @pl.when(chain & (hop[half] == 0))
        def _():
            y_copy(half, n, k, 0, True).start()
            y_copy(half, n, k, 1, True).start()
            y_local(half, n, k).start()

    def y_chain(half, n, k):
        @pl.when(jnp.logical_not(chain) | (hop[half] != 0))
        def _():
            y_copy(half, n, k, 0, False).wait_recv()

        @pl.when(chain & (hop[half] > 0))
        def _():
            @pl.when(hop[half] < 3)
            def _():
                y_copy(half, n, k, 0, False).start()

            y_copy(half, n, k, 1, False).start()

    def y_drain(half, n, k):
        @pl.when(chain & (hop[half] == 0))
        def _():
            y_local(half, n, k).wait()

        @pl.when(chain & (hop[half] < 3))
        def _():
            y_copy(half, n, k, 0, False).wait_send()

        @pl.when(chain)
        def _():
            y_copy(half, n, k, 1, False).wait_send()

    def factor(lo, hi):
        for q in range(lo, hi):
            k, part = q // 4, q % 4
            if q == 0:
                for d in range(1, NC):
                    p3(d).wait_recv()
                build_g(
                    pv[0].reshape(256, 256), pv[1].reshape(256, 256), pv[2].reshape(256, 256),
                    link_ref[0].astype(F32), g_ref,
                )
            if part == 0:
                diag_begin(k, g_ref, s_ref)
            panels(s_ref, part * 4, part * 4 + 4)
            if part == 3:
                diag_end(k, g_ref, s_ref, l_ref, v_ref)

    both = (0, 1)
    for h in both:
        rs_start(h, 0)
    factor(0, 3)
    for h in both:
        rs_middle(h, 0)
    factor(3, 6)
    for h in both:
        rs_end(h, 0)
        rs_start(h, 1)
    factor(6, 7)
    for h in both:
        rs_middle(h, 1)
    factor(7, 8)
    for h, own, o_ref, p_ref in ((0, own_a, oa_ref, pa), (1, own_b, ob_ref, pb)):
        rs_end(h, 1)
        keep = pltpu.make_async_copy(p_ref.at[:, :, x, z], o_ref.at[:, :, x, z], loc.at[h, 4])
        keep.start()
        keep.wait()
        ag_start(h, 0)
    factor(8, 9)
    for h in both:
        ag_forward(h, 0)
    factor(9, 10)
    for h in both:
        ag_wait(h, 0, (1, 3, 4, 5))
        ag_start(h, 1)
        y_source(h, (x, z)[h], 0)
    factor(10, 12)
    for h in both:
        ag_forward(h, 1)
    for h in both:
        y_chain(h, (x, z)[h], 0)
    factor(12, 14)
    for h in both:
        n = (x, z)[h]
        ag_wait(h, 1, (1,))
        y_source(h, n + 3, 1)
        ag_wait(h, 1, (3,))
        y_source(h, n + 1, 2)
    factor(14, 16)
    for h in both:
        n = (x, z)[h]
        y_chain(h, n + 3, 1)
        y_chain(h, n + 1, 2)
    for h in both:
        n = (x, z)[h]
        ag_wait(h, 1, (4, 5))
        y_source(h, n + 2, 3)
    for h in both:
        y_chain(h, (x, z)[h] + 2, 3)

    for h in both:
        n = (x, z)[h]
        for k, m in enumerate((n, n + 3, n + 1, n + 2)):
            y_drain(h, m, k)
        for phase in (0, 1):
            rs_drain(h, phase)
            ag_drain(h, phase)
    for d in range(1, NR):
        a2a(d).wait_send()
    for b, (sr, sc) in enumerate(sources):

        @pl.when((r == sr) & (c == sc))
        def _():
            for d in range(1, NC):
                p1(b, d).wait_send()

    for k in (0, 1):

        @pl.when(r == k)
        def _():
            for d in range(1, NR):
                p2(k, d).wait_send()

    for d in range(1, NC):
        p3(d).wait_send()


def move(live, link, dest, lrow, coup, hcol):
    vm = pl.BlockSpec(memory_space=pltpu.VMEM)
    sm = pl.BlockSpec(memory_space=pltpu.SMEM)
    hb = pl.BlockSpec(memory_space=pl.ANY)
    dma = pltpu.SemaphoreType.DMA
    half = jax.ShapeDtypeStruct((2, 5, NX, NZ, 16, 256), F32)
    cols = jax.ShapeDtypeStruct((5, NX, NZ, 16, 256), F32)
    square = jax.ShapeDtypeStruct((512, 512), F32)
    return pl.pallas_call(
        move_kernel,
        out_shape=(half, half, cols, cols, square, square),
        in_specs=[sm, sm, vm, vm, vm, vm],
        out_specs=[hb, hb, hb, hb, vm, vm],
        scratch_shapes=[
            pltpu.VMEM((NR, 72, 512), F32),
            pltpu.VMEM((NR, 72, 512), F32),
            pltpu.VMEM((512, 512), BF),
            pltpu.VMEM((512, 512), BF),
            pltpu.VMEM((3, NC, 16, 256), F32),
            pltpu.VMEM((NC, 16, 256), F32),
            pltpu.VMEM((2, 5, NX, NZ, 16, 256), F32),
            pltpu.VMEM((2, 5, NX, NZ, 16, 256), F32),
            pltpu.VMEM((6, 5, 4, 16, 256), F32),
            pltpu.VMEM((6, 5, 4, 16, 256), F32),
            pltpu.VMEM((6, 5, 16, 256), F32),
            pltpu.VMEM((6, 5, 16, 256), F32),
            pltpu.VMEM((8, 128), F32),
            pltpu.VMEM((8, 128), F32),
            pltpu.VMEM((512, 512), F32),
            pltpu.VMEM((128, 256), F32),
            dma((NR,)), dma((NR,)),
            dma((3, NC)), dma((3,)),
            dma((2, NR)), dma((2,)),
            dma((NC,)), dma((NC,)),
            dma((2, 2, 6)), dma((2, 2, 6)),
            dma((2, 2, 6)), dma((2, 2, 6)),
            dma((2, 4, 2)), dma((2, 4)),
            dma((2, 5)),
        ],
        compiler_params=pltpu.CompilerParams(
            collective_id=0, has_side_effects=True, vmem_limit_bytes=48 * 1024 * 1024
        ),
        name="move",
    )(live, link, dest, lrow, coup, hcol)


def update_kernel(
    where_ref, pat_ref, aa_ref, ab_ref, ja_ref, jb_ref, l_ref, v_ref, hess_ref, o_ref,
    v_s, wj_s,
):
    t = pl.program_id(0)
    r, c = where_ref[0], where_ref[1]

    def solve(a0, a1):
        h0, l0 = split(a0)
        h1, l1 = split(a1)
        w0 = dot1(jnp.concatenate([h0, l0, h0], 1), v_s[0:256, 0:768], 1, 1)
        w1 = dot1(jnp.concatenate([h0, l0, h0, h1, l1, h1], 1), v_s[256:512, :], 1, 1)
        return w0, w1

    @pl.when(t == 0)
    def _():
        for k in (0, 1):
            hi, lo = split(v_ref[:, k * 256 : (k + 1) * 256])
            v_s[:, k * 768 : (k + 1) * 768] = jnp.concatenate([hi, hi, lo], 1)
        for u in range(5):
            j = u * NC + c
            w0, w1 = solve(
                ja_ref[u] * pat_ref[j, 0].astype(F32), jb_ref[u] * pat_ref[j, 1].astype(F32)
            )
            h0, l0 = split(w0)
            h1, l1 = split(w1)
            wj_s[u] = jnp.concatenate([h0, l0, h0, h1, l1, h1], 1)

    i = t * NR + r
    w0, w1 = solve(
        aa_ref[0, 0] * pat_ref[i, 0].astype(F32), ab_ref[0, 0] * pat_ref[i, 1].astype(F32)
    )
    h0, l0 = split(w0)
    h1, l1 = split(w1)
    wi = jnp.concatenate([h0, h0, l0, h1, h1, l1], 1)

    def put(u, value):
        for h in range(2):
            o_ref[pl.Slice(2 * u + h, 256, 10), :] = value[:, h * 128 : (h + 1) * 128]

    for u in range(5):
        j = u * NC + c
        panel = j < 2

        @pl.when((i >= j) & jnp.logical_not(panel))
        def _():
            tile = hess_ref[0, u].astype(F32)
            upd = dot1(wi, wj_s[u], 1, 1)

            @pl.when(i == j)
            def _():
                put(u, sym_block(tile) - upd)

            @pl.when(i != j)
            def _():
                put(u, tile * pat_ref[i, j].astype(F32) - upd)

        @pl.when((i < j) & jnp.logical_not(panel))
        def _():
            put(u, jnp.zeros((256, 256), F32))

        if u == 0:

            @pl.when(panel & (i >= 2))
            def _():
                put(u, jnp.where(c == 0, w0, w1))

            @pl.when(panel & (i < 2))
            def _():
                rows = pl.ds(pl.multiple_of(i * 256, 256), 256)
                lcol = jnp.where(c == 0, l_ref[rows, 0:256], l_ref[rows, 256:512])
                put(u, lcol)


def update(where, pattern, oa, ob, ja, jb, lo, v, hess):
    panel = pl.BlockSpec((1, 1, 256, 256), lambda t: (t % 2, t // 2, 0, 0))
    full = lambda *shape: pl.BlockSpec(shape, lambda t: (0,) * len(shape))
    sm = pl.BlockSpec(memory_space=pltpu.SMEM)
    return pl.pallas_call(
        update_kernel,
        grid=(10,),
        out_shape=jax.ShapeDtypeStruct((25600, 128), F32),
        in_specs=[
            sm, sm, panel, panel, full(5, 256, 256), full(5, 256, 256),
            full(512, 512), full(512, 512),
            pl.BlockSpec((1, 5, 256, 256), lambda t: (t, 0, 0, 0)),
        ],
        out_specs=pl.BlockSpec((2560, 128), lambda t: (t, 0)),
        scratch_shapes=[pltpu.VMEM((512, 1536), BF), pltpu.VMEM((5, 256, 1536), BF)],
        compiler_params=pltpu.CompilerParams(vmem_limit_bytes=48 * 1024 * 1024),
        name="update",
    )(where, pattern, oa, ob, ja, jb, lo, v, hess)


def shards(hess, coupling, dest_row, local_row, live, pattern):
    blocks = jnp.transpose(hess[:, 0, :, :, 0, :], (0, 2, 1, 3))
    where = jnp.stack([lax.axis_index("row"), lax.axis_index("col")]).astype(jnp.int32)
    oa, ob, ja, jb, lo, v = move(
        live, pattern[1, 0].reshape(1), dest_row.reshape(1, 256), local_row,
        coupling.reshape(256, 512), blocks[:, 0],
    )
    out = update(
        where, pattern, oa.reshape(2, 5, 256, 256), ob.reshape(2, 5, 256, 256),
        ja.reshape(5, 256, 256), jb.reshape(5, 256, 256), lo, v, blocks,
    )
    return out.reshape(10, 1, 256, 5, 1, 256)


def solution(mesh):
    return jax.shard_map(
        shards,
        mesh=mesh,
        in_specs=(
            P(None, "row", None, None, "col", None),
            P(("row", "col"), None, None, None),
            P(("row", "col"), None, None),
            P(("row", "col"), None),
            P(("row", "col")),
            P(),
        ),
        out_specs=P(None, "row", None, None, "col", None),
        check_vma=False,
    )
```

time: 545 us -> 214 us (0.39); the launches traced: 535 us -> 212 us
  Pallas kernels: 0 us -> 207 us
  other arithmetic: 205 us -> 0.08 us
  local copies, waits for them, and re-layouts: 145 us -> 4.78 us
  waiting for transfers between devices: 106 us -> 0 us
  matrix products: 50.3 us -> 0 us
  between operations: 19 us -> 0.7 us
  starting transfers between devices: 9.81 us -> 0 us
    pallas_call x0 -> x2, Pallas kernels: none -> 207 us  [the longest x1 182 us: move(): pl.pallas_call(move_kernel, out_shape=(half, half, cols, cols, square, sq...]
    another operation x26 -> x1, other arithmetic: 113 us -> 0.08 us  [shards(): jnp.stack([lax.axis_index('row'), lax.axis_index('col')]).astype(jnp.int32)]
    psum x3 -> x0, waiting for transfers between devices: 106 us -> none  [the longest x1 102 us: shards(): lax.psum(jnp.stack([at_first * corner, at_below * corner, at_second * cor...]
    scatter-add x1 -> x0, other arithmetic: 63.4 us -> none  [shards(): partial_value = jnp.zeros((height, 2, block), jnp.float32).at[arrived_row...]
    scatter x3 -> x0, local copies, waits for them, and re-layouts: 36.2 us -> none  [the longest x1 24.4 us: shards(): outgoing = jnp.zeros((grid_rows * bucket, 2, block), jnp.float32).at[plac...]
    dot_general x3 -> x0, matrix products: 35.2 us -> none  [the longest x1 30.4 us: shards(): jnp.dot(left, right.T, precision=lax.Precision.HIGHEST)]
    mul x5 -> x0, other arithmetic: 19.8 us -> none  [the longest x1 11.6 us: shards(): links[:, :, None, None] * tiles]
    unnamed x28 -> x7, local copies, waits for them, and re-layouts: 18.3 us -> 1.09 us
  transfers between devices with their start and end apart: 5 -> 0, of which waited for: 2 -> 0; matrix products, arithmetic and copies ran while one was open for 45% -> 0% of each run, Pallas kernels for 0% -> 0%
where the time goes in v1:
time: 214 us; the launch traced here: 212 us
  Pallas kernels  207 us (97%)
  local copies, waits for them, and re-layouts  4.78 us (2%)
    pallas_call x1, Pallas kernels, move(): pl.pallas_call(move_kernel, out_shape=(half, half, cols, cols, square, sq...  182 us
    pallas_call x1, Pallas kernels, update(): pl.pallas_call(update_kernel, grid=(10,), out_shape=jax.ShapeDtypeStruct(...  24.7 us

profile of v1, /device:TPU:27, one launch (start us, length us, event | category | flops | bytes accessed | tf_op | source)
XLA Modules:
  0.0 212.2 jit_solution(17285508059695716250)
XLA Ops:
  0.0 0.0 copy-start.2
  0.0 0.0 copy-start.1
  0.7 0.1 pad_add_fusion.where_ref
  0.8 1.2 slice.6
  2.0 0.0 copy-start
  2.0 1.1 copy.9
  3.1 2.5 %slice_bitcast_fusion.hcol_ref = bf16[10,256,256]{2,1,0:T(8,128)(2,1)} fusion(bf16[10,5,256,256]{3,2,1,0:T(8,128)(2,1)} %bitcast.21), kind=kLoop, calls=%fused_computation | loop fusion | bytes 2621440 | tf_op jit(solution)/shard_map/squeeze | solution.py:615
  5.5 0.0 copy-done.2
  5.5 0.0 copy-done.1
  5.5 182.0 %move.1 = (f32[2,5,4,4,16,256]{5,4,3,2,1,0:T(8,128)}, f32[2,5,4,4,16,256]{5,4,3,2,1,0:T(8,128)}, f32[5,4,4,16,256]{4,3,2,1,0:T(8,128)S(1)}, f32[5,4,4,16,256]{4,...) custom-call(s32[1]{0:T(128)S(6)} %copy.10.live_ref, s32[1]{0:T(128)} %bitcast.2.link_ref, ...), custom_call_target="tpu_custom_call" | custom-call | tf_op jit(solution)/shard_map/move/pallas_call | solution.py:478
  187.5 0.0 copy-done
  187.6 24.7 %update.1 = f32[25600,128]{1,0:T(8,128)} custom-call(s32[2]{0:T(128)S(1)} %pad_add_fusion.where_ref, s32[80,80]{1,0:T(8,128)S(1)} %copy-done, f32[2,5,256,256]{3,2,1,0:T(8,128)} %bitcast.23, f32[2,5,256,256]{3,2,1,0:T(8,128)} %bitcast.24, f32[5,256,256]{2,1,0:T(8,128)S(1)} %bitcast.18, f32[5,256,256]{2,1,0:T(8,128)S(1)} %bitcast.19, ...), custom_call_target="tpu_custom_call" | custom-call | tf_op jit(solution)/shard_map/update/pallas_call | solution.py:594
Async XLA Ops:
  0.0 5.5 %copy-start.2 = (s32[1,256]{1,0:T(1,128)S(1)}, s32[1,256]{1,0:T(1,128)}, u32[]{:S(2)}) copy-start(s32[1,256]{1,0:T(1,128)} %lrow_ref.1) | copy-start | bytes 3076
  0.0 5.5 %copy-start.1 = (s32[1,256,1]{1,2,0:T(1,128)S(1)}, s32[1,256,1]{1,2,0:T(1,128)}, u32[]{:S(2)}) copy-start(s32[1,256,1]{1,2,0:T(1,128)} %param.8) | copy-start | bytes 3076
  2.0 185.6 %copy-start = (s32[80,80]{1,0:T(8,128)S(1)}, s32[80,80]{1,0:T(8,128)}, u32[]{:S(2)}) copy-start(s32[80,80]{1,0:T(8,128)} %pat_ref.1) | copy-start | bytes 76804

commit v2 on v1

v2 whole, which is shorter than its diff:
```python
import jax
import jax.numpy as jnp
from jax import lax
from jax.experimental import pallas as pl
from jax.experimental.pallas import tpu as pltpu
from jax.sharding import PartitionSpec as P

F32 = jnp.float32
BF = jnp.bfloat16
MESH = pl.DeviceIdType.MESH
NR, NC, NX, NZ = 8, 16, 4, 4


def dotg(a, b, ca, cb, precision=lax.Precision.HIGHEST):
    return lax.dot_general(
        a, b, (((ca,), (cb,)), ((), ())), precision=precision, preferred_element_type=F32
    )


def dot1(a, b, ca, cb):
    return lax.dot_general(a, b, (((ca,), (cb,)), ((), ())), preferred_element_type=F32)


def split(x):
    hi = x.astype(BF)
    return hi, (x - hi.astype(F32)).astype(BF)


def iota(shape, dim):
    return lax.broadcasted_iota(jnp.int32, shape, dim)


def sym_block(x):
    n = x.shape[0]
    return jnp.where(iota((n, n), 0) >= iota((n, n), 1), x, x.T)


def build_g(h00, h10, h11, link, g_ref):
    g_ref[0:256, 0:256] = sym_block(h00)
    g_ref[256:512, 256:512] = sym_block(h11)
    x = h10 * link
    g_ref[256:512, 0:256] = x
    g_ref[0:256, 256:512] = x.T
    for i in range(4):
        rows = slice(i * 128, (i + 1) * 128)
        g = g_ref[rows, :]
        on = iota((128, 512), 0) + i * 128 == iota((128, 512), 1)
        s = jnp.sum(jnp.where(on, 0.0, jnp.abs(g)), axis=1, keepdims=True) + 1.0
        g_ref[rows, :] = jnp.where(on, s, g)


def panels(s_ref, lo, hi):
    lane = iota((8, 128), 1)
    sub = iota((8, 1), 0)

    def body(b, carry):
        base = pl.multiple_of(b * 8, 8)
        rows = s_ref[pl.ds(base, 8), :]
        ra = rows[:, :128]
        cs = [
            jnp.sum(jnp.where(lane == base + j, ra, 0.0), axis=1, keepdims=True)
            for j in range(8)
        ]
        invd = jnp.zeros((8, 1), F32)
        for j in range(8):
            inv = 1.0 / cs[j][j : j + 1, :]
            m = jnp.where(sub > j, cs[j] * inv, 0.0)
            invd = jnp.where(sub == j, inv, invd)
            rows = rows - m * rows[j : j + 1, :]
            for k in range(j + 1, 8):
                cs[k] = cs[k] - m * cs[k][j : j + 1, :]
        s_ref[pl.ds(base, 8), :] = rows
        um = jnp.where(lane >= base + 8, rows[:, :128], 0.0)
        s_ref[...] = s_ref[...] - dotg(um, rows * invd, 0, 0)
        return carry

    lax.fori_loop(lo, hi, body, 0)


def diag_begin(k, g_ref, s_ref):
    o = k * 128
    s_ref[:, 0:128] = g_ref[o : o + 128, o : o + 128]
    s_ref[:, 128:256] = jnp.where(iota((128, 128), 0) == iota((128, 128), 1), 1.0, 0.0)


def diag_end(k, g_ref, s_ref, l_ref, v_ref):
    o, e = k * 128, k * 128 + 128
    r, c = iota((128, 128), 0), iota((128, 128), 1)
    u = s_ref[:, 0:128]
    s = lax.rsqrt(jnp.sum(jnp.where(r == c, u, 0.0), axis=1, keepdims=True))
    l_ref[o:e, o:e] = jnp.where(r <= c, u * s, 0.0).T
    v = s_ref[:, 128:256] * s
    v_ref[o:e, o:e] = v
    if e < 512:
        lp = dotg(g_ref[e:512, o:e], v, 1, 1)
        l_ref[e:512, o:e] = lp
        l_ref[o:e, e:512] = jnp.zeros((128, 512 - e), F32)
        v_ref[o:e, e:512] = jnp.zeros((128, 512 - e), F32)
        g_ref[e:512, e:512] = g_ref[e:512, e:512] - dotg(lp, lp, 1, 1)
    if o > 0:
        t = dotg(l_ref[o:e, 0:o], v_ref[0:o, 0:o], 1, 0)
        v_ref[o:e, 0:o] = -dotg(v, t, 1, 0)


def move_kernel(
    live_ref, link_ref, dest_ref, lrow_ref, coup_ref, hess_ref, *refs
):
    o_refs, j_refs, refs = refs[0:4], refs[4:8], refs[8:]
    (l_ref, v_ref, pack_s0, pack_s1, pack_r0, pack_r1, picks, hcol_ref, pv, pv2, pv_src), refs = (
        refs[:11],
        refs[11:],
    )
    pack_s, pack_r = (pack_s0, pack_s1), (pack_r0, pack_r1)
    p_refs, first_buf, second_buf, refs = refs[0:4], refs[4:8], refs[8:12], refs[12:]
    g_ref, s_ref = refs[:2]
    (
        a2a_s, a2a_r, p1_s, p1_r, p2_s, p2_r, p3_s, p3_r, p4_s, p4_r,
        rs_s, rs_r, ag_s, ag_r, y_s, y_r, loc, hload,
    ) = refs[2:]
    r = lax.axis_index("row")
    c = lax.axis_index("col")
    x, z = c // NZ, c % NZ
    side = r % 2
    twin = r + 1 - 2 * side
    par = c // NR

    def copy(src, dst, ss, rs, dev):
        return pltpu.make_async_remote_copy(
            src_ref=src, dst_ref=dst, send_sem=ss, recv_sem=rs, device_id=dev,
            device_id_type=MESH,
        )

    barrier = pltpu.get_barrier_semaphore()
    for d in range(1, NR):
        pl.semaphore_signal(barrier, 1, device_id=((r + d) % NR, c), device_id_type=MESH)
    for d in range(1, NC):
        pl.semaphore_signal(barrier, 1, device_id=(r, (c + d) % NC), device_id_type=MESH)
    load = pltpu.make_async_copy(hess_ref.at[:, 0], hcol_ref, hload)
    load.start()

    lane = iota((1, 256), 1)
    active = lane < live_ref[0]
    dest = dest_ref[...]
    hits = jnp.where((iota((NR, 256), 0) == dest) & active, 1.0, 0.0)
    before = jnp.where(iota((256, 256), 0) <= iota((256, 256), 1), 1.0, 0.0).astype(BF)
    cum = dot1(hits.astype(BF), before, 1, 0)
    rank = jnp.sum(hits * cum, axis=0, keepdims=True).astype(jnp.int32) - 1
    place = jnp.where(active, dest * 64 + rank, -1)
    pick = jnp.where(iota((512, 256), 0) == place, 1.0, 0.0).astype(BF)
    lr = lrow_ref[...]
    spot = jnp.where(iota((512, 256), 0) == rank + r * 64, 1.0, 0.0).astype(BF)
    lab_hi = (hits * (lr // 256).astype(F32)).astype(BF)
    lab_lo = (hits * (lr % 256).astype(F32)).astype(BF)
    labels = (
        dot1(lab_hi, spot, 1, 1) * 256.0
        + dot1(lab_lo, spot, 1, 1)
        + dot1(hits.astype(BF), spot, 1, 1)
    )
    for g in range(NR):
        pack_s[0][g, 64:72, :] = jnp.where(
            iota((8, 256), 0) == 0, labels[g : g + 1, 0:256], labels[g : g + 1, 256:512]
        )

    def pack(k):
        rows = jnp.concatenate(
            [coup_ref[pl.Slice(2 * h + k, 256, 4), :] for h in range(2)], axis=1
        )
        c_hi, c_lo = split(rows)
        packed = dot1(pick, c_hi, 1, 0) + dot1(pick, c_lo, 1, 0)
        pack_s[k][:, 0:64, :] = packed.reshape(NR, 64, 256)

    def a2a(k, d):
        to = (r + d) % NR
        return copy(
            pack_s[k].at[to], pack_r[k].at[r], a2a_s.at[k, d], a2a_r.at[k, d], (to, c)
        )

    far_first = (4, 3, 5, 2, 6, 1, 7)
    pack(0)
    pl.semaphore_wait(barrier, NR - 1 + NC - 1)
    for d in far_first:
        a2a(0, d).start()
    pack_r[0][r] = pack_s[0][r]
    pack(1)
    for d in far_first:
        a2a(1, d).start()
    pack_r[1][r] = pack_s[1][r]

    sources = ((0, 0), (1, 0), (1, 1))

    def p1(b, d):
        to = (sources[b][1] + d) % NC
        return copy(pv_src.at[to], pv.at[b, to], p1_s.at[b, d], p1_r.at[b], (sources[b][0], to))

    load.wait()
    pv_src[...] = hcol_ref[0].astype(F32).reshape(NC, 16, 256)
    for b, (sr, sc) in enumerate(sources):

        @pl.when((r == sr) & (c == sc))
        def _():
            for d in range(1, NC):
                p1(b, d).start()
            pv[b, sc] = pv_src[sc]

    def p2(k, d):
        blocks = pl.ds(0, 1) if k == 0 else pl.ds(1, 2)
        to = (k + d) % NR
        part = pv.at[blocks, c]
        return copy(part, part, p2_s.at[k, d], p2_r.at[k], (to, c))

    def p2_start():
        for b, (sr, sc) in enumerate(sources):

            @pl.when((r == sr) & (c != sc))
            def _():
                p1(b, 1).wait_recv()

        for k in (0, 1):

            @pl.when(r == k)
            def _():
                for d in range(1, NR):
                    p2(k, d).start()

    eight = pl.ds(pl.multiple_of(8 * side, 8), 8)

    def p3(d):
        return copy(
            pv.at[:, c, eight], pv2.at[:, c, eight], p3_s.at[d], p3_r.at[d], (r, (c + d) % NC)
        )

    def p3_start():
        for k in (0, 1):

            @pl.when(r != k)
            def _():
                p2(k, 1).wait_recv()

        for d in range(1, NC):
            p3(d).start()
        pv2[:, c, eight] = pv[:, c, eight]

    def p4():
        part = pv2.at[:, :, eight]
        return copy(part, part, p4_s, p4_r, (twin, c))

    def p4_start():
        for d in range(1, NC):
            p3(d).wait_recv()
        p4().start()

    def labels_in():
        lab = jnp.zeros((8, 256), F32)
        for g in range(NR):
            lab = lab + pack_r[0][g, 64:72, :]
        return jnp.concatenate([lab[0:1], lab[1:2]], axis=1).astype(jnp.int32) - 1

    def picks_in(lab, p):
        for t2 in range(5):
            t = 2 * t2 + p
            pick = jnp.where(iota((256, 512), 0) + t * 256 == lab, 1.0, 0.0).astype(BF)
            picks[p, t2 * 256 : t2 * 256 + 256, :] = pick

    def fill(k, p):
        rows = jnp.concatenate([pack_r[k][g, 0:64, :] for g in range(NR)], axis=0)
        hi, lo = split(rows)
        mine = jnp.where(c == k, 1.0, 0.0)
        got = dot1(picks[p], hi, 1, 0) + dot1(picks[p], lo, 1, 0)
        for t2 in range(5):
            part = got[t2 * 256 : t2 * 256 + 256] + hcol_ref[2 * t2 + p].astype(F32) * mine
            for h in range(2):
                p_refs[2 * k + h][p, t2] = part[:, h * 128 : (h + 1) * 128].reshape(
                    NX, NZ, 16, 128
                )

    def along_x(n):
        return (r, (n % NX) * NZ + z)

    def along_z(n):
        return (r, x * NZ + n % NZ)

    def unit(ref, g, big, n, p):
        n = n % 4
        if g % 2 == 0:
            return ref.at[p, :, n] if big else ref.at[p, :, x, n]
        return ref.at[p, :, :, n] if big else ref.at[p, :, n, z]

    def ring(g, big):
        return (x, along_x) if (g % 2 == 0) == big else (z, along_z)

    def rs(g, phase, m):
        n, dev = ring(g, phase == 0)
        buf = (first_buf, second_buf)[phase][g]
        at, p, to = (
            (n + 2, 0, n + 1), (n + 1, 1, n + 1), (n + 1, 0, n + 1),
            (n + 2, 1, n + 3), (n + 3, 0, n + 3), (n + 3, 1, n + 3),
        )[m]
        return copy(
            unit(p_refs[g], g, phase == 0, at, p), buf.at[m],
            rs_s.at[g, phase, m], rs_r.at[g, phase, m], dev(to),
        )

    def rs_start(k, phase, p):
        for m in ((0, 4), (3, 1))[p]:
            for g in (2 * k, 2 * k + 1):
                rs(g, phase, m).start()

    def rs_middle(k, phase):
        for m_in, m_out, step, p in ((0, 2, 1, 0), (3, 5, 3, 1)):
            for g in (2 * k, 2 * k + 1):
                n, dev = ring(g, phase == 0)
                rs(g, phase, m_in).wait_recv()
                ref = unit(p_refs[g], g, phase == 0, n + step, p)
                ref[...] = ref[...] + (first_buf, second_buf)[phase][g][m_in]
                rs(g, phase, m_out).start()

    def rs_end(k, phase):
        for p, (m1, m2) in enumerate(((4, 2), (1, 5))):
            for g in (2 * k, 2 * k + 1):
                n, dev = ring(g, phase == 0)
                buf = (first_buf, second_buf)[phase][g]
                rs(g, phase, m1).wait_recv()
                rs(g, phase, m2).wait_recv()
                ref = unit(p_refs[g], g, phase == 0, n, p)
                ref[...] = ref[...] + (buf[m1] + buf[m2])
            if phase == 0:
                rs_start(k, 1, p)

    def ag(g, phase, m):
        n, dev = ring(g, phase == 1)
        want = (lambda i: 0) if phase == 0 else (lambda i: i % 4 // 2) if g % 2 == 0 else (lambda i: par)
        back = want(n) if phase == 1 and g % 2 == 0 else 1 - want(n)
        at, p, to = (
            (n, want(n + 1), n + 1), (n, 1 - want(n + 1), n + 1), (n, want(n + 3), n + 3),
            (n, 1 - want(n + 3), n + 3), (n + 3, want(n), n + 1), (n + 1, back, n + 3),
        )[m]
        src = unit(o_refs[g], g, phase == 1, at, p)
        return copy(src, src, ag_s.at[g, phase, m], ag_r.at[g, phase, m], dev(to))

    def ag_own(k):
        keeps = [
            pltpu.make_async_copy(
                p_refs[g].at[:, :, x, z], o_refs[g].at[:, :, x, z], loc.at[g, 4]
            )
            for g in (2 * k, 2 * k + 1)
        ]
        for keep in keeps:
            keep.start()
        for keep in keeps:
            keep.wait()

    def ag_start(k):
        for m in (0, 3, 1, 2):
            for g in (2 * k, 2 * k + 1):
                ag(g, 0, m).start()

    def ag_forward(k):
        for m_in, m_out in ((0, 4), (3, 5)):
            for g in (2 * k, 2 * k + 1):
                ag(g, 0, m_in).wait_recv()
                ag(g, 0, m_out).start()

    def big_start(k):
        for m in (1, 2, 4, 5):
            for g in (2 * k, 2 * k + 1):
                ag(g, 0, m).wait_recv()
        for m in (0, 2):
            for g in (2 * k, 2 * k + 1):
                ag(g, 1, m).start()
        y_source(k, 0)

    def big_forward(k):
        for g in (2 * k, 2 * k + 1):
            ag(g, 1, 0).wait_recv()
            ag(g, 1, 4).start()
        for g in (2 * k, 2 * k + 1):
            ag(g, 1, 2).wait_recv()
            if g % 2 == 0:
                ag(g, 1, 5).start()
            ag(g, 1, 3).start()
            ag(g, 1, 1).start()
        y_source(k, 1)
        y_source(k, 2)

    def big_last(k):
        ag(2 * k, 1, 4).wait_recv()
        ag(2 * k, 1, 5).wait_recv()
        ag(2 * k + 1, 1, 4).wait_recv()
        y_source(k, 3)
        ag(2 * k + 1, 1, 3).wait_recv()
        ag(2 * k + 1, 1, 5).start()

    def big_end(k):
        ag(2 * k, 1, 1).wait_recv()
        ag(2 * k, 1, 3).wait_recv()
        ag(2 * k + 1, 1, 1).wait_recv()
        ag(2 * k + 1, 1, 5).wait_recv()

    y, ys = r // 2, (c % NR) // 2
    chain = side == c % 2
    hop = ((y - ys + 4) % 4, (ys - y + 4) % 4)

    def piece(g, i):
        return ring(g, True)[0] + (0, 3, 1, 2)[i]

    def y_refs(g, i):
        n = piece(g, i) % 4
        if g % 2 == 0:
            return o_refs[g].at[par, :, n], j_refs[g].at[:, n]
        return o_refs[g].at[par, :, :, n], j_refs[g].at[:, :, n]

    def y_copy(g, i, to_twin, from_o):
        o, j = y_refs(g, i)
        step = 2 if g % 2 == 0 else 6
        to = twin if to_twin else (r + step) % NR
        return copy(
            o if from_o else j, j, y_s.at[g, i, to_twin], y_r.at[g, i], (to, c)
        )

    def y_local(g, i):
        o, j = y_refs(g, i)
        return pltpu.make_async_copy(o, j, loc.at[g, i])

    def y_source(k, i):
        for g in (2 * k, 2 * k + 1):

            @pl.when(chain & (hop[g % 2] == 0))
            def _():
                y_copy(g, i, 0, True).start()
                y_copy(g, i, 1, True).start()
                y_local(g, i).start()

    def y_step(k, step):
        for far in (1, 2, 3):
            for g in (2 * k, 2 * k + 1):
                i = step - far
                if 0 <= i < 4:

                    @pl.when(chain & (hop[g % 2] == far))
                    def _():
                        y_copy(g, i, 0, False).wait_recv()
                        if far < 3:
                            y_copy(g, i, 0, False).start()
                        y_copy(g, i, 1, False).start()

    def y_last(k):
        for g in (2 * k, 2 * k + 1):
            for i in range(4):

                @pl.when(jnp.logical_not(chain))
                def _():
                    y_copy(g, i, 0, False).wait_recv()

                @pl.when(chain & (hop[g % 2] == 0))
                def _():
                    y_local(g, i).wait()

                @pl.when(chain & (hop[g % 2] < 3))
                def _():
                    y_copy(g, i, 0, False).wait_send()

                @pl.when(chain)
                def _():
                    y_copy(g, i, 1, False).wait_send()

    done = []

    def f(count):
        for _ in range(count):
            q = len(done)
            done.append(q)
            k, part = q // 8, q % 8
            if q == 0:
                p4().wait_recv()
                build_g(
                    pv2[0].reshape(256, 256), pv2[1].reshape(256, 256),
                    pv2[2].reshape(256, 256), link_ref[0].astype(F32), g_ref,
                )
            if part == 0:
                diag_begin(k, g_ref, s_ref)
            panels(s_ref, part * 2, part * 2 + 2)
            if part == 7:
                diag_end(k, g_ref, s_ref, l_ref, v_ref)

    def e0(k):
        for d in range(1, NR):
            a2a(k, d).wait_recv()
        if k == 0:
            lab = labels_in()
        for p in (0, 1):
            if k == 0:
                picks_in(lab, p)
            fill(k, p)
            rs_start(k, 0, p)

    p2_start()
    e0(0)
    p3_start()
    e0(1)
    rs_middle(0, 0)
    p4_start()
    f(2)
    rs_end(0, 0)
    rs_middle(1, 0)
    f(1)
    rs_middle(0, 1)
    f(1)
    rs_end(0, 1)
    ag_own(0)
    ag_start(0)
    f(2)
    ag_forward(0)
    rs_end(1, 0)
    f(1)
    big_start(0)
    rs_middle(1, 1)
    f(2)
    rs_end(1, 1)
    ag_own(1)
    ag_start(1)
    big_forward(0)
    f(1)
    y_step(0, 1)
    ag_forward(1)
    f(1)
    big_start(1)
    y_step(0, 2)
    f(1)
    big_last(0)
    y_step(0, 3)
    big_forward(1)
    y_step(1, 1)
    y_step(0, 4)
    f(2)
    y_step(0, 5)
    y_step(1, 2)
    f(1)
    big_last(1)
    f(3)
    y_step(0, 6)
    big_end(0)
    y_step(1, 3)
    f(4)
    y_step(1, 4)
    f(4)
    y_step(1, 5)
    f(4)
    y_step(1, 6)
    f(2)
    big_end(1)
    for k in (0, 1):
        y_last(k)

    for g in range(4):
        for phase in (0, 1):
            for m in range(6):
                rs(g, phase, m).wait_send()
                ag(g, phase, m).wait_send()
    for k in (0, 1):
        for d in range(1, NR):
            a2a(k, d).wait_send()
    for b, (sr, sc) in enumerate(sources):

        @pl.when((r == sr) & (c == sc))
        def _():
            for d in range(1, NC):
                p1(b, d).wait_send()

    for k in (0, 1):

        @pl.when(r == k)
        def _():
            for d in range(1, NR):
                p2(k, d).wait_send()

    for d in range(1, NC):
        p3(d).wait_send()
    p4().wait_send()


def move(live, link, dest, lrow, coup, blocks):
    vm = pl.BlockSpec(memory_space=pltpu.VMEM)
    sm = pl.BlockSpec(memory_space=pltpu.SMEM)
    hb = pl.BlockSpec(memory_space=pltpu.HBM)
    dma = pltpu.SemaphoreType.DMA
    group = jax.ShapeDtypeStruct((2, 5, NX, NZ, 16, 128), F32)
    cols = jax.ShapeDtypeStruct((5, NX, NZ, 16, 128), F32)
    square = jax.ShapeDtypeStruct((512, 512), F32)
    return pl.pallas_call(
        move_kernel,
        out_shape=(group,) * 4 + (cols,) * 4 + (square, square),
        in_specs=[sm, sm, vm, vm, vm, hb],
        out_specs=[vm] * 10,
        scratch_shapes=[
            pltpu.VMEM((NR, 72, 256), F32),
            pltpu.VMEM((NR, 64, 256), F32),
            pltpu.VMEM((NR, 72, 256), F32),
            pltpu.VMEM((NR, 64, 256), F32),
            pltpu.VMEM((2, 1280, 512), BF),
            pltpu.VMEM((10, 256, 256), BF),
            pltpu.VMEM((3, NC, 16, 256), F32),
            pltpu.VMEM((3, NC, 16, 256), F32),
            pltpu.VMEM((NC, 16, 256), F32),
        ]
        + [pltpu.VMEM((2, 5, NX, NZ, 16, 128), F32)] * 4
        + [pltpu.VMEM((6, 5, 4, 16, 128), F32)] * 4
        + [pltpu.VMEM((6, 5, 16, 128), F32)] * 4
        + [
            pltpu.VMEM((512, 512), F32),
            pltpu.VMEM((128, 256), F32),
            dma((2, NR)), dma((2, NR)),
            dma((3, NC)), dma((3,)),
            dma((2, NR)), dma((2,)),
            dma((NC,)), dma((NC,)),
            dma(()), dma(()),
            dma((4, 2, 6)), dma((4, 2, 6)),
            dma((4, 2, 6)), dma((4, 2, 6)),
            dma((4, 4, 2)), dma((4, 4)),
            dma((4, 5)), dma(()),
        ],
        compiler_params=pltpu.CompilerParams(
            collective_id=0, has_side_effects=True, vmem_limit_bytes=40 * 1024 * 1024
        ),
        name="move",
    )(live, link, dest, lrow, coup, blocks)


def update_kernel(
    where_ref, pat_ref, a0_ref, a1_ref, a2_ref, a3_ref, j0_ref, j1_ref, j2_ref, j3_ref,
    l_ref, v_ref, hess_ref, o_ref, v_s, wj_s,
):
    s = pl.program_id(0)
    r, c = where_ref[0], where_ref[1]

    def wide(left, right):
        return jnp.concatenate([left, right], axis=1)

    def solve(a0, a1):
        h0, l0 = split(a0)
        h1, l1 = split(a1)
        w0 = dot1(jnp.concatenate([h0, l0, h0], 1), v_s[0:256, 0:768], 1, 1)
        w1 = dot1(jnp.concatenate([h0, l0, h0, h1, l1, h1], 1), v_s[256:512, :], 1, 1)
        return w0, w1

    @pl.when(s == 0)
    def _():
        for k in (0, 1):
            hi, lo = split(v_ref[:, k * 256 : (k + 1) * 256])
            v_s[:, k * 768 : (k + 1) * 768] = jnp.concatenate([hi, hi, lo], 1)

        def column(u, carry):
            j = u * NC + c
            w0, w1 = solve(
                wide(j0_ref[u], j1_ref[u]) * pat_ref[j, 0].astype(F32),
                wide(j2_ref[u], j3_ref[u]) * pat_ref[j, 1].astype(F32),
            )
            h0, l0 = split(w0)
            h1, l1 = split(w1)
            wj_s[u] = jnp.concatenate([h0, l0, h0, h1, l1, h1], 1)
            return carry

        lax.fori_loop(0, 5, column, 0)

    rows = (s * 2 * NR + r, s * 2 * NR + NR + r)

    def links(k):
        return jnp.where(
            iota((512, 1), 0) < 256, pat_ref[rows[0], k], pat_ref[rows[1], k]
        ).astype(F32)

    def pair(left, right):
        return wide(left[:, s].reshape(512, 128), right[:, s].reshape(512, 128))

    w0, w1 = solve(pair(a0_ref, a1_ref) * links(0), pair(a2_ref, a3_ref) * links(1))
    h0, l0 = split(w0)
    h1, l1 = split(w1)
    wi = jnp.concatenate([h0, h0, l0, h1, h1, l1], 1)

    def put(p, u, value):
        for h in range(2):
            o_ref[pl.Slice(2560 * p + 2 * u + h, 256, 10), :] = value[:, h * 128 : (h + 1) * 128]

    for u in range(5):
        j = u * NC + c
        panel = j < 2

        @pl.when((u < s) & jnp.logical_not(panel))
        def _():
            upd = dot1(wi, wj_s[u], 1, 1)
            for p in (0, 1):
                tile = hess_ref[2 * s + p, u].astype(F32)
                put(p, u, tile * pat_ref[rows[p], j].astype(F32) - upd[p * 256 : p * 256 + 256])

        for p in (0, 1):
            i = rows[p]

            @pl.when((u == s) & (i >= j) & jnp.logical_not(panel))
            def _():
                tile = hess_ref[2 * s + p, u].astype(F32)
                upd = dot1(wi[p * 256 : p * 256 + 256], wj_s[u], 1, 1)

                @pl.when(i == j)
                def _():
                    put(p, u, sym_block(tile) - upd)

                @pl.when(i != j)
                def _():
                    put(p, u, tile * pat_ref[i, j].astype(F32) - upd)

            @pl.when((i < j) & jnp.logical_not(panel))
            def _():
                put(p, u, jnp.zeros((256, 256), F32))

            if u == 0:

                @pl.when(panel & (i >= 2))
                def _():
                    put(p, u, jnp.where(c == 0, w0, w1)[p * 256 : p * 256 + 256])

                if p == 0:

                    @pl.when(panel & (i < 2))
                    def _():
                        at = pl.ds(pl.multiple_of(i * 256, 256), 256)
                        put(p, u, jnp.where(c == 0, l_ref[at, 0:256], l_ref[at, 256:512]))


def update(where, pattern, moved, hess):
    vm = pl.BlockSpec(memory_space=pltpu.VMEM)
    sm = pl.BlockSpec(memory_space=pltpu.SMEM)
    return pl.pallas_call(
        update_kernel,
        grid=(5,),
        out_shape=jax.ShapeDtypeStruct((25600, 128), F32),
        in_specs=[sm, sm] + [vm] * 11,
        out_specs=pl.BlockSpec((5120, 128), lambda s: (s, 0)),
        scratch_shapes=[pltpu.VMEM((512, 1536), BF), pltpu.VMEM((5, 256, 1536), BF)],
        compiler_params=pltpu.CompilerParams(vmem_limit_bytes=20 * 1024 * 1024),
        name="update",
    )(
        where, pattern, *[o.reshape(2, 5, 256, 128) for o in moved[0:4]],
        *[j.reshape(5, 256, 128) for j in moved[4:8]], *moved[8:], hess,
    )


def shards(hess, coupling, dest_row, local_row, live, pattern):
    blocks = jnp.transpose(hess[:, 0, :, :, 0, :], (0, 2, 1, 3))
    where = jnp.stack([lax.axis_index("row"), lax.axis_index("col")]).astype(jnp.int32)
    coup = jnp.transpose(coupling.reshape(256, 2, 2, 128), (0, 2, 1, 3)).reshape(1024, 128)
    moved = move(
        live, pattern[1, 0].reshape(1), dest_row.reshape(1, 256), local_row, coup, blocks
    )
    out = update(where, pattern, moved, blocks)
    return out.reshape(10, 1, 256, 5, 1, 256)


def solution(mesh):
    return jax.shard_map(
        shards,
        mesh=mesh,
        in_specs=(
            P(None, "row", None, None, "col", None),
            P(("row", "col"), None, None, None),
            P(("row", "col"), None, None),
            P(("row", "col"), None),
            P(("row", "col")),
            P(),
        ),
        out_specs=P(None, "row", None, None, "col", None),
        check_vma=False,
    )
```

time: 214 us -> 140 us (0.65)
  Pallas kernels: 207 us -> 134 us
    pallas_call x2, Pallas kernels: 207 us -> 134 us  [the longest x1 113 us: move(): pl.pallas_call(move_kernel, out_shape=(group,) * 4 + (cols,) * 4 + (squar...]
    squeeze x1 -> x0, local copies, waits for them, and re-layouts: 2.46 us -> none  [shards(): blocks[:, 0]]
where the time goes in v2:
time: 140 us; the launch traced here: 138 us
  Pallas kernels  134 us (96%)
  local copies, waits for them, and re-layouts  3.6 us (3%)
    pallas_call x1, Pallas kernels, move(): pl.pallas_call(move_kernel, out_shape=(group,) * 4 + (cols,) * 4 + (squar...  113 us
    pallas_call x1, Pallas kernels, update(): pl.pallas_call(update_kernel, grid=(5,), out_shape=jax.ShapeDtypeStruct((...  21.3 us

profile of v2, /device:TPU:27, one launch (start us, length us, event | category | flops | bytes accessed | tf_op | source)
XLA Modules:
  0.0 138.2 jit_solution(12110299033811676379)
XLA Ops:
  0.7 0.1 pad_add_fusion.where_ref
  0.7 1.2 slice.3
  1.9 0.0 copy-start.1
  1.9 1.0 copy-done.1
  3.0 0.0 copy-start.3
  3.0 0.7 copy-done.3
  3.6 0.0 copy-start.4
  3.7 0.7 copy-done.4
  4.3 0.0 copy-start
  4.3 0.0 copy-start.2
  4.3 112.5 %move.1 = (f32[2,5,4,4,16,128]{5,4,3,2,1,0:T(8,128)S(1)}, f32[2,5,4,4,16,128]{5,4,3,2,1,0:T(8,128)S(1)}, f32[2,5,4,4,16,128]{5,4,3,2,1,0:T(8,128)S(1)}, f32[2,5,...) custom-call(s32[1]{0:T(128)S(6)} %copy.11.live_ref, ...), custom_call_target="tpu_custom_call" | custom-call | tf_op jit(solution)/shard_map/move/pallas_call | solution.py:589
  116.9 0.0 copy-done
  116.9 0.0 copy-done.2
  116.9 21.3 %update.1 = f32[25600,128]{1,0:T(8,128)} custom-call(s32[2]{0:T(128)S(1)} %pad_add_fusion.where_ref, s32[80,80]{1,0:T(8,128)S(1)} %copy-done.2, f32[2,5,256,128]{3,2,1,0:T(8,128)S(1)} %bitcast.23, f32[2,5,256,128]{3,2,1,0:T(8,128)S(1)} %bitcast.24, f32[2,5,256,128]{3,2,1,0:T(8,128)S(1)} %bitcast.25, f32[2,5,256,128]{3,2,1,0:T(8,128)S(1)} %bitcast.26, ...), custom_call_target="tpu_custom_call" | custom-call | tf_op jit(solution)/shard_map/update/pallas_call | solution.py:731
Async XLA Ops:
  1.9 1.0 copy-start.1
  3.0 0.7 copy-start.3
  3.6 0.7 copy-start.4
  4.3 112.5 %copy-start = (bf16[10,1,256,5,1,256]{5,2,4,3,1,0:T(8,128)(2,1)S(1)}, bf16[10,1,256,5,1,256]{5,2,4,3,1,0:T(8,128)(2,1)}, u32[]{:S(2)}) copy-start(bf16[10,1,256,5,1,256]{5,2,4,3,1,0:T(8,128)(2,1)} %param.6) | copy-start | bytes 19660804
  4.3 112.6 %copy-start.2 = (s32[80,80]{1,0:T(8,128)S(1)}, s32[80,80]{1,0:T(8,128)}, u32[]{:S(2)}) copy-start(s32[80,80]{1,0:T(8,128)} %pat_ref.1) | copy-start | bytes 76804

commit v3 on v2

--- a/solution.py
+++ b/solution.py
@@ -103,7 +103,7 @@
 
 
 def move_kernel(
-    live_ref, link_ref, dest_ref, lrow_ref, coup_ref, hess_ref, *refs
+    live_ref, pat_hbm, dest_hbm, lrow_hbm, coup_hbm, hess_ref, *refs
 ):
     o_refs, j_refs, refs = refs[0:4], refs[4:8], refs[8:]
     (l_ref, v_ref, pack_s0, pack_s1, pack_r0, pack_r1, picks, hcol_ref, pv, pv2, pv_src), refs = (
@@ -112,11 +112,11 @@
     )
     pack_s, pack_r = (pack_s0, pack_s1), (pack_r0, pack_r1)
     p_refs, first_buf, second_buf, refs = refs[0:4], refs[4:8], refs[8:12], refs[12:]
-    g_ref, s_ref = refs[:2]
+    g_ref, s_ref, pat_ref, dest_ref, lrow_ref, coup_ref, lead_ref = refs[:7]
     (
         a2a_s, a2a_r, p1_s, p1_r, p2_s, p2_r, p3_s, p3_r, p4_s, p4_r,
         rs_s, rs_r, ag_s, ag_r, y_s, y_r, loc, hload,
-    ) = refs[2:]
+    ) = refs[7:]
     r = lax.axis_index("row")
     c = lax.axis_index("col")
     x, z = c // NZ, c % NZ
@@ -135,8 +135,23 @@
         pl.semaphore_signal(barrier, 1, device_id=((r + d) % NR, c), device_id_type=MESH)
     for d in range(1, NC):
         pl.semaphore_signal(barrier, 1, device_id=(r, (c + d) % NC), device_id_type=MESH)
-    load = pltpu.make_async_copy(hess_ref.at[:, 0], hcol_ref, hload)
-    load.start()
+    loads = [
+        pltpu.make_async_copy(src, dst, hload.at[i])
+        for i, (src, dst) in enumerate(
+            (
+                (dest_hbm, dest_ref),
+                (lrow_hbm, lrow_ref),
+                (coup_hbm, coup_ref),
+                (hess_ref.at[0, 0], lead_ref),
+                (pat_hbm, pat_ref),
+                (hess_ref.at[:, 0], hcol_ref),
+            )
+        )
+    ]
+    for load in loads:
+        load.start()
+    for load in loads[:4]:
+        load.wait()
 
     lane = iota((1, 256), 1)
     active = lane < live_ref[0]
@@ -176,15 +191,9 @@
         )
 
     far_first = (4, 3, 5, 2, 6, 1, 7)
+    pv_src[...] = lead_ref[...].astype(F32).reshape(NC, 16, 256)
     pack(0)
     pl.semaphore_wait(barrier, NR - 1 + NC - 1)
-    for d in far_first:
-        a2a(0, d).start()
-    pack_r[0][r] = pack_s[0][r]
-    pack(1)
-    for d in far_first:
-        a2a(1, d).start()
-    pack_r[1][r] = pack_s[1][r]
 
     sources = ((0, 0), (1, 0), (1, 1))
 
@@ -192,8 +201,6 @@
         to = (sources[b][1] + d) % NC
         return copy(pv_src.at[to], pv.at[b, to], p1_s.at[b, d], p1_r.at[b], (sources[b][0], to))
 
-    load.wait()
-    pv_src[...] = hcol_ref[0].astype(F32).reshape(NC, 16, 256)
     for b, (sr, sc) in enumerate(sources):
 
         @pl.when((r == sr) & (c == sc))
@@ -202,6 +209,11 @@
                 p1(b, d).start()
             pv[b, sc] = pv_src[sc]
 
+    for d in far_first:
+        a2a(0, d).start()
+    pack_r[0][r] = pack_s[0][r]
+    pack(1)
+
     def p2(k, d):
         blocks = pl.ds(0, 1) if k == 0 else pl.ds(1, 2)
         to = (k + d) % NR
@@ -248,6 +260,14 @@
         for d in range(1, NC):
             p3(d).wait_recv()
         p4().start()
+
+    p2_start()
+    for d in far_first:
+        a2a(1, d).start()
+    pack_r[1][r] = pack_s[1][r]
+    p3_start()
+    loads[4].wait()
+    loads[5].wait()
 
     def labels_in():
         lab = jnp.zeros((8, 256), F32)
@@ -474,7 +494,7 @@
                 p4().wait_recv()
                 build_g(
                     pv2[0].reshape(256, 256), pv2[1].reshape(256, 256),
-                    pv2[2].reshape(256, 256), link_ref[0].astype(F32), g_ref,
+                    pv2[2].reshape(256, 256), pat_ref[1:2, 0:1].astype(F32), g_ref,
                 )
             if part == 0:
                 diag_begin(k, g_ref, s_ref)
@@ -493,25 +513,26 @@
             fill(k, p)
             rs_start(k, 0, p)
 
-    p2_start()
     e0(0)
-    p3_start()
+    p4_start()
     e0(1)
+    f(3)
     rs_middle(0, 0)
-    p4_start()
-    f(2)
+    f(3)
     rs_end(0, 0)
+    f(1)
     rs_middle(1, 0)
-    f(1)
+    f(2)
     rs_middle(0, 1)
-    f(1)
+    f(2)
     rs_end(0, 1)
     ag_own(0)
     ag_start(0)
     f(2)
     ag_forward(0)
+    f(1)
     rs_end(1, 0)
-    f(1)
+    f(2)
     big_start(0)
     rs_middle(1, 1)
     f(2)
@@ -522,31 +543,31 @@
     f(1)
     y_step(0, 1)
     ag_forward(1)
-    f(1)
+    f(2)
     big_start(1)
     y_step(0, 2)
     f(1)
     big_last(0)
     y_step(0, 3)
+    f(1)
     big_forward(1)
     y_step(1, 1)
     y_step(0, 4)
-    f(2)
+    f(1)
     y_step(0, 5)
     y_step(1, 2)
+    f(2)
+    big_last(1)
     f(1)
-    big_last(1)
-    f(3)
     y_step(0, 6)
     big_end(0)
     y_step(1, 3)
-    f(4)
+    f(2)
     y_step(1, 4)
-    f(4)
+    f(2)
     y_step(1, 5)
-    f(4)
+    f(1)
     y_step(1, 6)
-    f(2)
     big_end(1)
     for k in (0, 1):
         y_last(k)
@@ -578,7 +599,7 @@
     p4().wait_send()
 
 
-def move(live, link, dest, lrow, coup, blocks):
+def move(live, pattern, dest, lrow, coup, blocks):
     vm = pl.BlockSpec(memory_space=pltpu.VMEM)
     sm = pl.BlockSpec(memory_space=pltpu.SMEM)
     hb = pl.BlockSpec(memory_space=pltpu.HBM)
@@ -589,7 +610,7 @@
     return pl.pallas_call(
         move_kernel,
         out_shape=(group,) * 4 + (cols,) * 4 + (square, square),
-        in_specs=[sm, sm, vm, vm, vm, hb],
+        in_specs=[sm] + [hb] * 5,
         out_specs=[vm] * 10,
         scratch_shapes=[
             pltpu.VMEM((NR, 72, 256), F32),
@@ -608,6 +629,11 @@
         + [
             pltpu.VMEM((512, 512), F32),
             pltpu.VMEM((128, 256), F32),
+            pltpu.VMEM((80, 80), jnp.int32),
+            pltpu.VMEM((1, 256), jnp.int32),
+            pltpu.VMEM((1, 256), jnp.int32),
+            pltpu.VMEM((1024, 128), F32),
+            pltpu.VMEM((256, 256), BF),
             dma((2, NR)), dma((2, NR)),
             dma((3, NC)), dma((3,)),
             dma((2, NR)), dma((2,)),
@@ -616,13 +642,13 @@
             dma((4, 2, 6)), dma((4, 2, 6)),
             dma((4, 2, 6)), dma((4, 2, 6)),
             dma((4, 4, 2)), dma((4, 4)),
-            dma((4, 5)), dma(()),
+            dma((4, 5)), dma((6,)),
         ],
         compiler_params=pltpu.CompilerParams(
             collective_id=0, has_side_effects=True, vmem_limit_bytes=40 * 1024 * 1024
         ),
         name="move",
-    )(live, link, dest, lrow, coup, blocks)
+    )(live, pattern, dest, lrow, coup, blocks)
 
 
 def update_kernel(
@@ -748,7 +774,7 @@
     where = jnp.stack([lax.axis_index("row"), lax.axis_index("col")]).astype(jnp.int32)
     coup = jnp.transpose(coupling.reshape(256, 2, 2, 128), (0, 2, 1, 3)).reshape(1024, 128)
     moved = move(
-        live, pattern[1, 0].reshape(1), dest_row.reshape(1, 256), local_row, coup, blocks
+        live, pattern, dest_row.reshape(1, 256), local_row, coup, blocks
     )
     out = update(where, pattern, moved, blocks)
     return out.reshape(10, 1, 256, 5, 1, 256)

time: 140 us -> 135 us (0.964); the launches traced: 138 us -> 135 us
  Pallas kernels: 134 us -> 131 us
    pallas_call x1, Pallas kernels: 113 us -> 110 us  [move(): pl.pallas_call(move_kernel, out_shape=(group,) * 4 + (cols,) * 4 + (squar...]
where the time goes in v3:
time: 135 us
  Pallas kernels  131 us (97%)
  local copies, waits for them, and re-layouts  3.18 us (2%)
    pallas_call x1, Pallas kernels, move(): pl.pallas_call(move_kernel, out_shape=(group,) * 4 + (cols,) * 4 + (squar...  110 us
    pallas_call x1, Pallas kernels, update(): pl.pallas_call(update_kernel, grid=(5,), out_shape=jax.ShapeDtypeStruct((...  21.1 us
    unnamed x10, local copies, waits for them, and re-layouts  3.18 us

profile of v3, /device:TPU:27, one launch (start us, length us, event | category | flops | bytes accessed | tf_op | source)
XLA Modules:
  0.0 134.8 jit_solution(14026298407971339640)
XLA Ops:
  0.7 0.1 pad_add_fusion.where_ref
  0.7 0.0 copy-start.1
  0.7 1.0 copy-done.1
  1.8 0.0 copy-start.2
  1.8 0.8 copy-done.2
  2.5 0.0 copy-start.3
  2.6 0.7 copy-done.3
  3.2 0.0 copy-start.4
  3.2 0.7 copy-done.4
  3.9 0.0 copy-start
  3.9 109.8 %move.1 = (f32[2,5,4,4,16,128]{5,4,3,2,1,0:T(8,128)S(1)}, f32[2,5,4,4,16,128]{5,4,3,2,1,0:T(8,128)S(1)}, f32[2,5,4,4,16,128]{5,4,3,2,1,0:T(8,128)S(1)}, f32[2,5,...) custom-call(s32[1]{0:T(128)S(6)} %copy.11.live_ref, ...), custom_call_target="tpu_custom_call" | custom-call | tf_op jit(solution)/shard_map/move/pallas_call | solution.py:610
  113.8 0.0 copy-done
  113.8 21.1 %update.1 = f32[25600,128]{1,0:T(8,128)} custom-call(s32[2]{0:T(128)S(1)} %pad_add_fusion.where_ref, s32[80,80]{1,0:T(8,128)S(1)} %copy-done.2, f32[2,5,256,128]{3,2,1,0:T(8,128)S(1)} %bitcast.22, f32[2,5,256,128]{3,2,1,0:T(8,128)S(1)} %bitcast.23, f32[2,5,256,128]{3,2,1,0:T(8,128)S(1)} %bitcast.24, f32[2,5,256,128]{3,2,1,0:T(8,128)S(1)} %bitcast.25, ...), custom_call_target="tpu_custom_call" | custom-call | tf_op jit(solution)/shard_map/update/pallas_call | solution.py:757
Async XLA Ops:
  0.7 1.0 copy-start.1
  1.8 0.8 copy-start.2
  2.5 0.7 copy-start.3
  3.2 0.7 copy-start.4
  3.9 109.9 %copy-start = (bf16[10,1,256,5,1,256]{5,2,4,3,1,0:T(8,128)(2,1)S(1)}, bf16[10,1,256,5,1,256]{5,2,4,3,1,0:T(8,128)(2,1)}, u32[]{:S(2)}) copy-start(bf16[10,1,256,5,1,256]{5,2,4,3,1,0:T(8,128)(2,1)} %param.6) | copy-start | bytes 19660804

commit v4 on v3

--- a/solution.py
+++ b/solution.py
@@ -24,6 +24,12 @@
 def split(x):
     hi = x.astype(BF)
     return hi, (x - hi.astype(F32)).astype(BF)
+
+
+def split3(x):
+    hi = x.astype(BF).astype(F32)
+    mid = (x - hi).astype(BF).astype(F32)
+    return hi, mid, x - hi - mid
 
 
 def iota(shape, dim):
@@ -71,7 +77,10 @@
                 cs[k] = cs[k] - m * cs[k][j : j + 1, :]
         s_ref[pl.ds(base, 8), :] = rows
         um = jnp.where(lane >= base + 8, rows[:, :128], 0.0)
-        s_ref[...] = s_ref[...] - dotg(um, rows * invd, 0, 0)
+        u, w = split3(um), split3(rows * invd)
+        left = jnp.concatenate([u[i] for i in (0, 0, 1, 0, 2, 1)], axis=0).astype(BF)
+        right = jnp.concatenate([w[i] for i in (0, 1, 0, 2, 0, 1)], axis=0).astype(BF)
+        s_ref[...] = s_ref[...] - dot1(left, right, 0, 0)
         return carry
 
     lax.fori_loop(lo, hi, body, 0)
@@ -418,7 +427,7 @@
 
     y, ys = r // 2, (c % NR) // 2
     chain = side == c % 2
-    hop = ((y - ys + 4) % 4, (ys - y + 4) % 4)
+    hop = (y - ys + 4) % 4
 
     def piece(g, i):
         return ring(g, True)[0] + (0, 3, 1, 2)[i]
@@ -429,39 +438,43 @@
             return o_refs[g].at[par, :, n], j_refs[g].at[:, n]
         return o_refs[g].at[par, :, :, n], j_refs[g].at[:, :, n]
 
-    def y_copy(g, i, to_twin, from_o):
+    def y_copy(g, i, way, from_o=False):
         o, j = y_refs(g, i)
-        step = 2 if g % 2 == 0 else 6
-        to = twin if to_twin else (r + step) % NR
-        return copy(
-            o if from_o else j, j, y_s.at[g, i, to_twin], y_r.at[g, i], (to, c)
-        )
+        onward = 2 if g % 2 == 0 else 6
+        to = ((r + 2) % NR, twin, (r + 6) % NR, (r + onward) % NR)[way]
+        return copy(o if from_o else j, j, y_s.at[g, i, way], y_r.at[g, i], (to, c))
 
     def y_local(g, i):
         o, j = y_refs(g, i)
         return pltpu.make_async_copy(o, j, loc.at[g, i])
 
     def y_source(k, i):
-        for g in (2 * k, 2 * k + 1):
-
-            @pl.when(chain & (hop[g % 2] == 0))
-            def _():
-                y_copy(g, i, 0, True).start()
+        @pl.when(chain & (hop == 0))
+        def _():
+            for g in (2 * k, 2 * k + 1):
+                for way in ((0, 2), (2, 0))[g % 2]:
+                    y_copy(g, i, way, True).start()
+            for g in (2 * k, 2 * k + 1):
                 y_copy(g, i, 1, True).start()
                 y_local(g, i).start()
 
-    def y_step(k, step):
-        for far in (1, 2, 3):
-            for g in (2 * k, 2 * k + 1):
-                i = step - far
-                if 0 <= i < 4:
-
-                    @pl.when(chain & (hop[g % 2] == far))
-                    def _():
-                        y_copy(g, i, 0, False).wait_recv()
-                        if far < 3:
-                            y_copy(g, i, 0, False).start()
-                        y_copy(g, i, 1, False).start()
+    def near(k, i):
+        for far in (1, 3):
+
+            @pl.when(chain & (hop == far))
+            def _():
+                for g in (2 * k, 2 * k + 1) if far == 1 else (2 * k + 1, 2 * k):
+                    y_copy(g, i, 1).wait_recv()
+                    if (far == 1) == (g % 2 == 0):
+                        y_copy(g, i, 3).start()
+                    y_copy(g, i, 1).start()
+
+    def far(k, i):
+        @pl.when(chain & (hop == 2))
+        def _():
+            for g in (2 * k, 2 * k + 1):
+                y_copy(g, i, 1).wait_recv()
+                y_copy(g, i, 1).start()
 
     def y_last(k):
         for g in (2 * k, 2 * k + 1):
@@ -469,19 +482,21 @@
 
                 @pl.when(jnp.logical_not(chain))
                 def _():
-                    y_copy(g, i, 0, False).wait_recv()
-
-                @pl.when(chain & (hop[g % 2] == 0))
+                    y_copy(g, i, 1).wait_recv()
+
+                @pl.when(chain & (hop == 0))
                 def _():
                     y_local(g, i).wait()
-
-                @pl.when(chain & (hop[g % 2] < 3))
+                    y_copy(g, i, 0).wait_send()
+                    y_copy(g, i, 2).wait_send()
+
+                @pl.when(chain & (hop == (1 if g % 2 == 0 else 3)))
                 def _():
-                    y_copy(g, i, 0, False).wait_send()
+                    y_copy(g, i, 3).wait_send()
 
                 @pl.when(chain)
                 def _():
-                    y_copy(g, i, 1, False).wait_send()
+                    y_copy(g, i, 1).wait_send()
 
     done = []
 
@@ -516,9 +531,9 @@
     e0(0)
     p4_start()
     e0(1)
-    f(3)
+    f(4)
     rs_middle(0, 0)
-    f(3)
+    f(4)
     rs_end(0, 0)
     f(1)
     rs_middle(1, 0)
@@ -540,35 +555,38 @@
     ag_own(1)
     ag_start(1)
     big_forward(0)
-    f(1)
-    y_step(0, 1)
+    f(2)
+    near(0, 0)
     ag_forward(1)
     f(2)
     big_start(1)
-    y_step(0, 2)
+    far(0, 0)
+    near(0, 1)
     f(1)
     big_last(0)
-    y_step(0, 3)
+    near(0, 2)
     f(1)
     big_forward(1)
-    y_step(1, 1)
-    y_step(0, 4)
+    far(0, 1)
+    near(1, 0)
     f(1)
-    y_step(0, 5)
-    y_step(1, 2)
+    near(0, 3)
+    far(0, 2)
+    f(1)
+    big_last(1)
+    far(0, 3)
+    far(1, 0)
+    near(1, 1)
+    f(1)
+    big_end(0)
+    near(1, 2)
+    f(1)
+    far(1, 1)
+    near(1, 3)
     f(2)
-    big_last(1)
-    f(1)
-    y_step(0, 6)
-    big_end(0)
-    y_step(1, 3)
-    f(2)
-    y_step(1, 4)
-    f(2)
-    y_step(1, 5)
-    f(1)
-    y_step(1, 6)
+    far(1, 2)
     big_end(1)
+    far(1, 3)
     for k in (0, 1):
         y_last(k)
 
@@ -641,7 +659,7 @@
             dma(()), dma(()),
             dma((4, 2, 6)), dma((4, 2, 6)),
             dma((4, 2, 6)), dma((4, 2, 6)),
-            dma((4, 4, 2)), dma((4, 4)),
+            dma((4, 4, 4)), dma((4, 4)),
             dma((4, 5)), dma((6,)),
         ],
         compiler_params=pltpu.CompilerParams(
@@ -674,18 +692,21 @@
             hi, lo = split(v_ref[:, k * 256 : (k + 1) * 256])
             v_s[:, k * 768 : (k + 1) * 768] = jnp.concatenate([hi, hi, lo], 1)
 
-        def column(u, carry):
-            j = u * NC + c
-            w0, w1 = solve(
-                wide(j0_ref[u], j1_ref[u]) * pat_ref[j, 0].astype(F32),
-                wide(j2_ref[u], j3_ref[u]) * pat_ref[j, 1].astype(F32),
-            )
-            h0, l0 = split(w0)
-            h1, l1 = split(w1)
-            wj_s[u] = jnp.concatenate([h0, l0, h0, h1, l1, h1], 1)
-            return carry
-
-        lax.fori_loop(0, 5, column, 0)
+        def masks(k):
+            out = jnp.zeros((1280, 1), F32)
+            for u in range(5):
+                out = jnp.where(
+                    iota((1280, 1), 0) // 256 == u, pat_ref[u * NC + c, k].astype(F32), out
+                )
+            return out
+
+        def tall(left, right):
+            return wide(left[...].reshape(1280, 128), right[...].reshape(1280, 128))
+
+        w0, w1 = solve(tall(j0_ref, j1_ref) * masks(0), tall(j2_ref, j3_ref) * masks(1))
+        h0, l0 = split(w0)
+        h1, l1 = split(w1)
+        wj_s[...] = jnp.concatenate([h0, l0, h0, h1, l1, h1], 1).reshape(5, 256, 1536)
 
     rows = (s * 2 * NR + r, s * 2 * NR + NR + r)
 
@@ -761,7 +782,7 @@
         in_specs=[sm, sm] + [vm] * 11,
         out_specs=pl.BlockSpec((5120, 128), lambda s: (s, 0)),
         scratch_shapes=[pltpu.VMEM((512, 1536), BF), pltpu.VMEM((5, 256, 1536), BF)],
-        compiler_params=pltpu.CompilerParams(vmem_limit_bytes=20 * 1024 * 1024),
+        compiler_params=pltpu.CompilerParams(vmem_limit_bytes=30 * 1024 * 1024),
         name="update",
     )(
         where, pattern, *[o.reshape(2, 5, 256, 128) for o in moved[0:4]],

time: 135 us -> 129 us (0.956)
  the two profiles are of different devices: /device:TPU:27 before, /device:TPU:3 now
where the time goes in v4:
time: 129 us
  Pallas kernels  125 us (97%)
  local copies, waits for them, and re-layouts  3.18 us (2%)
    pallas_call x1, Pallas kernels, move(): pl.pallas_call(move_kernel, out_shape=(group,) * 4 + (cols,) * 4 + (squar...  107 us
    pallas_call x1, Pallas kernels, update(): pl.pallas_call(update_kernel, grid=(5,), out_shape=jax.ShapeDtypeStruct((...  18.2 us
    unnamed x10, local copies, waits for them, and re-layouts  3.18 us

profile of v4, /device:TPU:3, one launch (start us, length us, event | category | flops | bytes accessed | tf_op | source)
XLA Modules:
  0.0 128.8 jit_solution(9931885594641395043)
XLA Ops:
  0.7 0.1 pad_add_fusion.where_ref
  0.7 0.0 copy-start.1
  0.7 1.0 copy-done.1
  1.8 0.0 copy-start.2
  1.8 0.8 copy-done.2
  2.5 0.0 copy-start.3
  2.6 0.7 copy-done.3
  3.2 0.0 copy-start.4
  3.2 0.7 copy-done.4
  3.9 0.0 copy-start
  3.9 106.7 %move.1 = (f32[2,5,4,4,16,128]{5,4,3,2,1,0:T(8,128)S(1)}, f32[2,5,4,4,16,128]{5,4,3,2,1,0:T(8,128)S(1)}, f32[2,5,4,4,16,128]{5,4,3,2,1,0:T(8,128)S(1)}, f32[2,5,...) custom-call(s32[1]{0:T(128)S(6)} %copy.11.live_ref, ...), custom_call_target="tpu_custom_call" | custom-call | tf_op jit(solution)/shard_map/move/pallas_call | solution.py:628
  110.6 0.0 copy-done
  110.7 18.2 %update.1 = f32[25600,128]{1,0:T(8,128)} custom-call(s32[2]{0:T(128)S(1)} %pad_add_fusion.where_ref, s32[80,80]{1,0:T(8,128)S(1)} %copy-done.2, f32[2,5,256,128]{3,2,1,0:T(8,128)S(1)} %bitcast.22, f32[2,5,256,128]{3,2,1,0:T(8,128)S(1)} %bitcast.23, f32[2,5,256,128]{3,2,1,0:T(8,128)S(1)} %bitcast.24, f32[2,5,256,128]{3,2,1,0:T(8,128)S(1)} %bitcast.25, ...), custom_call_target="tpu_custom_call" | custom-call | tf_op jit(solution)/shard_map/update/pallas_call | solution.py:778
Async XLA Ops:
  0.7 1.0 copy-start.1
  1.8 0.8 copy-start.2
  2.5 0.7 copy-start.3
  3.2 0.7 copy-start.4
  3.9 106.7 %copy-start = (bf16[10,1,256,5,1,256]{5,2,4,3,1,0:T(8,128)(2,1)S(1)}, bf16[10,1,256,5,1,256]{5,2,4,3,1,0:T(8,128)(2,1)}, u32[]{:S(2)}) copy-start(bf16[10,1,256,5,1,256]{5,2,4,3,1,0:T(8,128)(2,1)} %param.6) | copy-start | bytes 19660804

commit v5 on v4

--- a/solution.py
+++ b/solution.py
@@ -112,7 +112,7 @@
 
 
 def move_kernel(
-    live_ref, pat_hbm, dest_hbm, lrow_hbm, coup_hbm, hess_ref, *refs
+    live_ref, pat_hbm, dest_ref, lrow_ref, coup_ref, hess_ref, *refs
 ):
     o_refs, j_refs, refs = refs[0:4], refs[4:8], refs[8:]
     (l_ref, v_ref, pack_s0, pack_s1, pack_r0, pack_r1, picks, hcol_ref, pv, pv2, pv_src), refs = (
@@ -121,11 +121,11 @@
     )
     pack_s, pack_r = (pack_s0, pack_s1), (pack_r0, pack_r1)
     p_refs, first_buf, second_buf, refs = refs[0:4], refs[4:8], refs[8:12], refs[12:]
-    g_ref, s_ref, pat_ref, dest_ref, lrow_ref, coup_ref, lead_ref = refs[:7]
+    g_ref, s_ref, pat_ref, lead_ref = refs[:4]
     (
         a2a_s, a2a_r, p1_s, p1_r, p2_s, p2_r, p3_s, p3_r, p4_s, p4_r,
         rs_s, rs_r, ag_s, ag_r, y_s, y_r, loc, hload,
-    ) = refs[7:]
+    ) = refs[4:]
     r = lax.axis_index("row")
     c = lax.axis_index("col")
     x, z = c // NZ, c % NZ
@@ -148,9 +148,6 @@
         pltpu.make_async_copy(src, dst, hload.at[i])
         for i, (src, dst) in enumerate(
             (
-                (dest_hbm, dest_ref),
-                (lrow_hbm, lrow_ref),
-                (coup_hbm, coup_ref),
                 (hess_ref.at[0, 0], lead_ref),
                 (pat_hbm, pat_ref),
                 (hess_ref.at[:, 0], hcol_ref),
@@ -159,8 +156,6 @@
     ]
     for load in loads:
         load.start()
-    for load in loads[:4]:
-        load.wait()
 
     lane = iota((1, 256), 1)
     active = lane < live_ref[0]
@@ -200,8 +195,9 @@
         )
 
     far_first = (4, 3, 5, 2, 6, 1, 7)
+    pack(0)
+    loads[0].wait()
     pv_src[...] = lead_ref[...].astype(F32).reshape(NC, 16, 256)
-    pack(0)
     pl.semaphore_wait(barrier, NR - 1 + NC - 1)
 
     sources = ((0, 0), (1, 0), (1, 1))
@@ -275,8 +271,8 @@
         a2a(1, d).start()
     pack_r[1][r] = pack_s[1][r]
     p3_start()
-    loads[4].wait()
-    loads[5].wait()
+    loads[1].wait()
+    loads[2].wait()
 
     def labels_in():
         lab = jnp.zeros((8, 256), F32)
@@ -351,7 +347,11 @@
                 rs(g, phase, m1).wait_recv()
                 rs(g, phase, m2).wait_recv()
                 ref = unit(p_refs[g], g, phase == 0, n, p)
-                ref[...] = ref[...] + (buf[m1] + buf[m2])
+                total = ref[...] + (buf[m1] + buf[m2])
+                if phase == 0:
+                    ref[...] = total
+                else:
+                    o_refs[g][p, :, x, z] = total
             if phase == 0:
                 rs_start(k, 1, p)
 
@@ -365,18 +365,6 @@
         )[m]
         src = unit(o_refs[g], g, phase == 1, at, p)
         return copy(src, src, ag_s.at[g, phase, m], ag_r.at[g, phase, m], dev(to))
-
-    def ag_own(k):
-        keeps = [
-            pltpu.make_async_copy(
-                p_refs[g].at[:, :, x, z], o_refs[g].at[:, :, x, z], loc.at[g, 4]
-            )
-            for g in (2 * k, 2 * k + 1)
-        ]
-        for keep in keeps:
-            keep.start()
-        for keep in keeps:
-            keep.wait()
 
     def ag_start(k):
         for m in (0, 3, 1, 2):
@@ -531,59 +519,50 @@
     e0(0)
     p4_start()
     e0(1)
-    f(4)
+    f(6)
     rs_middle(0, 0)
-    f(4)
+    f(6)
     rs_end(0, 0)
-    f(1)
+    f(2)
     rs_middle(1, 0)
+    f(3)
+    rs_middle(0, 1)
+    f(3)
+    rs_end(0, 1)
+    ag_start(0)
+    f(3)
+    ag_forward(0)
     f(2)
-    rs_middle(0, 1)
-    f(2)
-    rs_end(0, 1)
-    ag_own(0)
-    ag_start(0)
-    f(2)
-    ag_forward(0)
-    f(1)
     rs_end(1, 0)
     f(2)
     big_start(0)
     rs_middle(1, 1)
     f(2)
     rs_end(1, 1)
-    ag_own(1)
     ag_start(1)
     big_forward(0)
     f(2)
     near(0, 0)
     ag_forward(1)
-    f(2)
+    f(1)
     big_start(1)
     far(0, 0)
     near(0, 1)
-    f(1)
     big_last(0)
     near(0, 2)
-    f(1)
     big_forward(1)
     far(0, 1)
     near(1, 0)
-    f(1)
     near(0, 3)
     far(0, 2)
-    f(1)
     big_last(1)
     far(0, 3)
     far(1, 0)
     near(1, 1)
-    f(1)
     big_end(0)
     near(1, 2)
-    f(1)
     far(1, 1)
     near(1, 3)
-    f(2)
     far(1, 2)
     big_end(1)
     far(1, 3)
@@ -628,7 +607,7 @@
     return pl.pallas_call(
         move_kernel,
         out_shape=(group,) * 4 + (cols,) * 4 + (square, square),
-        in_specs=[sm] + [hb] * 5,
+        in_specs=[sm, hb, vm, vm, vm, hb],
         out_specs=[vm] * 10,
         scratch_shapes=[
             pltpu.VMEM((NR, 72, 256), F32),
@@ -648,9 +627,6 @@
             pltpu.VMEM((512, 512), F32),
             pltpu.VMEM((128, 256), F32),
             pltpu.VMEM((80, 80), jnp.int32),
-            pltpu.VMEM((1, 256), jnp.int32),
-            pltpu.VMEM((1, 256), jnp.int32),
-            pltpu.VMEM((1024, 128), F32),
             pltpu.VMEM((256, 256), BF),
             dma((2, NR)), dma((2, NR)),
             dma((3, NC)), dma((3,)),
@@ -660,7 +636,7 @@
             dma((4, 2, 6)), dma((4, 2, 6)),
             dma((4, 2, 6)), dma((4, 2, 6)),
             dma((4, 4, 4)), dma((4, 4)),
-            dma((4, 5)), dma((6,)),
+            dma((4, 4)), dma((3,)),
         ],
         compiler_params=pltpu.CompilerParams(
             collective_id=0, has_side_effects=True, vmem_limit_bytes=40 * 1024 * 1024

time: 129 us -> 128 us (level)
  no operation moved by 1% of the time
where the time goes in v5:
time: 128 us
  Pallas kernels  124 us (97%)
  local copies, waits for them, and re-layouts  3.18 us (2%)
    pallas_call x1, Pallas kernels, move(): pl.pallas_call(move_kernel, out_shape=(group,) * 4 + (cols,) * 4 + (squar...  106 us
    pallas_call x1, Pallas kernels, update(): pl.pallas_call(update_kernel, grid=(5,), out_shape=jax.ShapeDtypeStruct((...  18.2 us
    unnamed x10, local copies, waits for them, and re-layouts  3.18 us

profile of v5, /device:TPU:3, one launch (start us, length us, event | category | flops | bytes accessed | tf_op | source)
XLA Modules:
  0.0 128.0 jit_solution(13015019997890351537)
XLA Ops:
  0.7 0.1 pad_add_fusion.where_ref
  0.7 0.0 copy-start.1
  0.7 1.0 copy-done.1
  1.8 0.0 copy-start.2
  1.8 0.8 copy-done.2
  2.5 0.0 copy-start.3
  2.6 0.7 copy-done.3
  3.2 0.0 copy-start.4
  3.2 0.7 copy-done.4
  3.9 0.0 copy-start
  3.9 105.9 %move.1 = (f32[2,5,4,4,16,128]{5,4,3,2,1,0:T(8,128)S(1)}, f32[2,5,4,4,16,128]{5,4,3,2,1,0:T(8,128)S(1)}, f32[2,5,4,4,16,128]{5,4,3,2,1,0:T(8,128)S(1)}, f32[2,5,...) custom-call(s32[1]{0:T(128)S(6)} %copy.11.live_ref, ...), custom_call_target="tpu_custom_call" | custom-call | tf_op jit(solution)/shard_map/move/pallas_call | solution.py:607
  109.8 0.0 copy-done
  109.8 18.2 %update.1 = f32[25600,128]{1,0:T(8,128)} custom-call(s32[2]{0:T(128)S(1)} %pad_add_fusion.where_ref, s32[80,80]{1,0:T(8,128)S(1)} %copy-done.2, f32[2,5,256,128]{3,2,1,0:T(8,128)S(1)} %bitcast.22, f32[2,5,256,128]{3,2,1,0:T(8,128)S(1)} %bitcast.23, f32[2,5,256,128]{3,2,1,0:T(8,128)S(1)} %bitcast.24, f32[2,5,256,128]{3,2,1,0:T(8,128)S(1)} %bitcast.25, ...), custom_call_target="tpu_custom_call" | custom-call | tf_op jit(solution)/shard_map/update/pallas_call | solution.py:754
Async XLA Ops:
  0.7 1.0 copy-start.1
  1.8 0.8 copy-start.2
  2.5 0.7 copy-start.3
  3.2 0.7 copy-start.4
  3.9 105.9 %copy-start = (bf16[10,1,256,5,1,256]{5,2,4,3,1,0:T(8,128)(2,1)S(1)}, bf16[10,1,256,5,1,256]{5,2,4,3,1,0:T(8,128)(2,1)}, u32[]{:S(2)}) copy-start(bf16[10,1,256,5,1,256]{5,2,4,3,1,0:T(8,128)(2,1)} %param.6) | copy-start | bytes 19660804
